TPU v7x, 32 devices: a whole 2x2x4 slice. The times are simulated.
32 devices in a mesh: row: 4 (over y, x), col: 8 (over z, core).
Axes of the slice: x: 2, y: 2, z: 4, core: 2. Of those that a mesh axis runs over, the one named last changes fastest.
Arguments:
- sectors: int32 [96], replicated, may hold values from 0 to 7
- environment: bfloat16 [24576, 24576], P('col', 'row'), may hold values from -0.109375 to 0.109375
- wavefunction: bfloat16 [24576, 2048], P('row', 'col'), may hold values from -6 to 6
Outputs:
- applied: bfloat16 [24576, 2048], P('col', 'row')
All inputs are finite; a program needn't handle non-finite values.
Results may differ from a plain program's by a relative error of at most 0.013.
Values may be sent and summed in bfloat16 or wider, within the bound.
No kernel may reach another device: no remote copies, remote signals or barrier semaphores. Data moves between devices by JAX's collectives and lax.ppermute only.
A program may use at most 192 MiB of HBM per device.

v0:
```python
import jax
import jax.numpy as jnp
from jax import lax
from jax.sharding import PartitionSpec as P

BLOCK = 256


def body(sectors, environment, wavefunction):
    row_tile, col_tile = environment.shape
    row_blocks = row_tile // BLOCK
    col_blocks = col_tile // BLOCK
    row_sector = lax.dynamic_slice_in_dim(sectors, lax.axis_index("col") * row_blocks, row_blocks)
    col_sector = lax.dynamic_slice_in_dim(sectors, lax.axis_index("row") * col_blocks, col_blocks)
    allowed = row_sector[:, None] == col_sector[None, :]
    allowed = jnp.repeat(jnp.repeat(allowed, BLOCK, axis=0), BLOCK, axis=1)
    masked = jnp.where(allowed, environment, jnp.zeros_like(environment))
    gathered = lax.all_gather(wavefunction, "col", axis=1, tiled=True)
    partial_value = jnp.dot(masked, gathered, preferred_element_type=jnp.float32)
    result = lax.psum_scatter(
        partial_value.astype(jnp.bfloat16), "row", scatter_dimension=1, tiled=True
    )
    return result


def solution(mesh):
    placed = (P(), P("col", "row"), P("row", "col"))
    return jax.shard_map(
        body, mesh=mesh, in_specs=placed, out_specs=P("col", "row"), check_vma=False
    )
```

profile of v0, /device:TPU:17, one launch (start us, length us, event | category | flops | bytes accessed | tf_op | source)
XLA Modules:
  0.0 448.0 jit_solution(5527713326037631243)
XLA Ops:
  6.5 0.0 all-gather.2.cloned.1.call-start
  6.5 0.7 all-gather.2.cloned.1.call-update
  7.3 0.0 reduce-scatter.2.cloned.1.call-start
  7.3 0.7 dynamic_slice.6
  8.0 0.7 dynamic_slice.7
  8.8 0.1 broadcast_compare_fusion
  8.8 0.1 broadcast_in_dim.11
  9.0 13.5 %broadcast_in_dim.12 = pred[3072,24,256]{2,1,0:T(8,128)(4,1)S(1)} broadcast(pred[3072,24]{1,0:T(8,128)(4,1)S(1)} %bitcast.7), dimensions={0,1} | broadcast | bytes 18948096 | tf_op jit(solution)/shard_map/broadcast_in_dim | solution.py:16
  22.4 23.6 %copy.4 = pred[384,8,24,256]{3,1,2,0:T(8,128)(4,1)} copy(pred[384,8,24,256]{3,2,1,0:T(8,128)(4,1)S(1)} %bitcast.5) | data formatting | bytes 37748736
  46.0 183.9 %all-gather.2.cloned.1.call-done = bf16[6144,2048]{1,0:T(8,128)(2,1)} async-done(((bf16[6144,256]{1,0:T(8,128)(2,1)}), bf16[6144,2048]{1,0:T(8,128)(2,1)}) %all-gather.2.cloned.1.call-update) | async-done | bytes 25165840 | tf_op jit(solution)/shard_map/all_gather | solution.py:18
  229.9 90.6 %fusion.3 = bf16[3072,2048]{1,0:T(8,128)(2,1)} fusion(bf16[6144,2048]{1,0:T(8,128)(2,1)} %all-gather.2.cloned.1.call-done, pred[3072,6144]{1,0:T(8,128)(4,1)} %bitcast.6, bf16[3072,6144]{1,0:T(8,128)(2,1)} %param.4), kind=kOutput, calls=%fused_computation.3 | convolution fusion | flops 77334577152 | bytes 94371840 | tf_op jit(solution)/shard_map/dot_general | solution.py:19
  320.4 0.0 reduce-scatter.2.cloned.1.call-update
  320.5 120.7 %reduce-scatter.2.cloned.1.call-done = bf16[3072,512]{1,0:T(8,128)(2,1)} async-done(((bf16[3072,2048]{1,0:T(8,128)(2,1)}), bf16[3072,512]{1,0:T(8,128)(2,1)}) %reduce-scatter.2.cloned.1.call-update) | async-done | bytes 3145744 | tf_op jit(solution)/shard_map/reduce_scatter | solution.py:20
Async XLA Ops:
  6.5 223.3 %all-gather.2.cloned.1.call-start = ((), (), s32[]{:S(2)}) async-start(), calls=%async_computation.1 | async-start | bytes 28311552 | tf_op jit(solution)/shard_map/all_gather | solution.py:18
  7.3 433.9 %reduce-scatter.2.cloned.1.call-start = ((), (), s32[]{:S(2)}) async-start(), calls=%async_computation.2 | async-start | bytes 15728640 | tf_op jit(solution)/shard_map/reduce_scatter | solution.py:20
Sparse Core Ops, SparseCore 0:
  8.9 220.8 all-gather.1
  320.6 120.5 reduce-scatter.1
where the time goes:
time: 450 us; the launch traced here: 448 us
  waiting for transfers between devices  305 us (68%)
  matrix products  90.6 us (20%)
  local copies, waits for them, and re-layouts  38.6 us (9%)
  between operations  13.4 us (3%)
    all_gather x1, waiting for transfers between devices, body(): gathered = lax.all_gather(wavefunction, 'col', axis=1, tiled=True)  184 us
    reduce_scatter x1, waiting for transfers between devices, body(): lax.psum_scatter(partial_value.astype(jnp.bfloat16), 'row', scatter_dimen...  121 us
    dot_general x1, matrix products, body(): jnp.dot(masked, gathered, preferred_element_type=jnp.float32)  90.6 us
    unnamed x1, local copies, waits for them, and re-layouts  23.6 us
    broadcast_in_dim x2, local copies, waits for them, and re-layouts, body(): allowed = jnp.repeat(jnp.repeat(allowed, BLOCK, axis=0), BLOCK, axis=1)  13.6 us
  transfers between devices with their start and end apart: 2, of which 2 were waited for; matrix products, arithmetic and copies ran while one was open for 9% of the time, Pallas kernels for 0%

commit v1 on v0

v1 whole, which is shorter than its diff:
```python
import functools

import jax
import jax.numpy as jnp
from jax import lax
from jax.experimental import pallas as pl
from jax.experimental.pallas import tpu as pltpu
from jax.sharding import PartitionSpec as P

BLOCK = 256
LANES = 128
SLOTS = 32
GROUP = 8
HIDING = 106 * 10**9
AXES = ("row", "col")
VMEM_BYTES = 60 * 1024 * 1024
TINY = pl.CostEstimate(flops=1, bytes_accessed=1, transcendentals=0)
TOKEN = jax.ShapeDtypeStruct((8, LANES), jnp.float32)
ANYWHERE = pl.BlockSpec(memory_space=pl.ANY)
SCALARS = pl.BlockSpec(memory_space=pltpu.SMEM)


def pair_kernel(row_blocks, col_blocks, bases_ref, sectors_ref, pairs_ref):
    def visit(step, count):
        i, j = step // col_blocks, step % col_blocks
        pairs_ref[1 + count] = i * 256 + j
        row = bases_ref[1 + i // row_blocks] + i % row_blocks
        same = sectors_ref[row] == sectors_ref[bases_ref[0] + j]
        return count + same.astype(jnp.int32)

    steps = (bases_ref.shape[0] - 1) * row_blocks * col_blocks
    pairs_ref[0] = lax.fori_loop(0, steps, visit, jnp.int32(0))


def block_pairs(sectors, row_blocks, col_blocks, cols):
    bases = jnp.stack([lax.axis_index("row") * col_blocks] + [col * row_blocks for col in cols]).astype(jnp.int32)
    return pl.pallas_call(
        functools.partial(pair_kernel, row_blocks, col_blocks),
        out_shape=jax.ShapeDtypeStruct((len(cols) * row_blocks * col_blocks + 1 + GROUP + SLOTS,), jnp.int32),
        in_specs=[SCALARS] * 2,
        out_specs=SCALARS,
        cost_estimate=TINY,
        name="block_pairs",
    )(bases, sectors)


def product_kernel(n_env, n_parts, n_old, n_out, writes, pairs_ref, at_ref, *refs):
    env_refs, part_refs = refs[:n_env], refs[n_env : n_env + 2 * n_parts]
    refs = refs[n_env + 2 * n_parts + n_old + 1 :]
    out_refs = refs[:n_out]
    wave, blocks, total, result, wave_sem, block_sem, out_sem = refs[n_out + 1 :]
    count = pairs_ref[0]
    row_blocks = env_refs[0].shape[0] // BLOCK

    def block_copy(step, env_ref, first):
        pair = pairs_ref[1 + step]
        rows = pl.ds(pl.multiple_of((pair // 256 - first) * BLOCK, BLOCK), BLOCK)
        source = env_ref.at[rows, pl.ds(pl.multiple_of(pair % 256 * BLOCK, BLOCK), BLOCK)]
        return pltpu.make_async_copy(source, blocks.at[step % SLOTS], block_sem.at[step % SLOTS])

    def fetch(step):
        i = pairs_ref[1 + step] // 256
        for n, env_ref in enumerate(env_refs):

            @pl.when((step < count) & (i >= n * row_blocks) & (i < (n + 1) * row_blocks))
            def _():
                block_copy(step, env_ref, n * row_blocks).start()

    waves, at = [], 0
    for k in range(n_parts):
        x_ref, y_ref = part_refs[2 * k : 2 * k + 2]
        target = wave.at[:, pl.ds(at, x_ref.shape[1])]
        waves.append(pltpu.make_async_copy(x_ref, target, wave_sem.at[k]))
        pl.when(at_ref[0] == 1)(waves[-1].start)
        pl.when(at_ref[0] == 0)(pltpu.make_async_copy(y_ref, target, wave_sem.at[k]).start)
        at += x_ref.shape[1]
    for step in range(SLOTS):
        fetch(step)

    total[...] = jnp.zeros_like(total)
    for copy in waves:
        copy.wait()

    spare = total.shape[0] // BLOCK - 1

    def visit(group, carry):
        steps = [group * GROUP + u for u in range(GROUP)]
        for step in steps:

            @pl.when(step < count)
            def _():
                source = env_refs[0].at[pl.ds(0, BLOCK), pl.ds(0, BLOCK)]
                pltpu.make_async_copy(source, blocks.at[step % SLOTS], block_sem.at[step % SLOTS]).wait()

        products = []
        for step in steps:
            real = step < count
            pair = pairs_ref[1 + step]
            i, j = jnp.where(real, pair // 256, spare), jnp.where(real, pair % 256, 0)
            rows = pl.ds(pl.multiple_of(i * BLOCK, BLOCK), BLOCK)
            depth = pl.ds(pl.multiple_of(j * BLOCK, BLOCK), BLOCK)
            products.append((rows, jnp.dot(blocks[step % SLOTS], wave[depth, :], preferred_element_type=jnp.float32)))
        for rows, product in products:
            total[rows, :] += product
        for step in steps:
            fetch(step + SLOTS)

        return carry

    lax.fori_loop(0, (count + GROUP - 1) // GROUP, visit, 0)
    result[...] = total[: result.shape[0], :].astype(result.dtype)
    copies = []
    for k, (start, size, top, height, target, tile) in enumerate(writes):
        there = pl.ds(pl.multiple_of(at_ref[tile], BLOCK) if tile else 0, height)
        source = result.at[pl.ds(top, height), pl.ds(start, size)]
        copies.append(pltpu.make_async_copy(source, out_refs[target].at[there, :], out_sem.at[k]))
        copies[-1].start()
    for copy in copies:
        copy.wait()


def block_product(pairs, at, environments, parts, old, new, writes, after, flops=1):
    rows, depth = environments[0].shape
    rows, width, n_env = rows * len(environments), sum(x.shape[1] for x, _ in parts), len(environments)
    results = pl.pallas_call(
        functools.partial(product_kernel, n_env, len(parts), len(old), len(old) + len(new), writes),
        out_shape=[jax.ShapeDtypeStruct(z.shape, z.dtype) for z in (*old, *new)] + [TOKEN],
        in_specs=[SCALARS] * 2 + [ANYWHERE] * (n_env + 2 * len(parts) + 1 + len(old)),
        out_specs=[ANYWHERE] * (len(old) + len(new) + 1),
        scratch_shapes=[
            pltpu.VMEM((depth, width), jnp.bfloat16),
            pltpu.VMEM((SLOTS, BLOCK, BLOCK), jnp.bfloat16),
            pltpu.VMEM((rows + BLOCK, width), jnp.float32),
            pltpu.VMEM((rows, width), jnp.bfloat16),
            pltpu.SemaphoreType.DMA((len(parts),)),
            pltpu.SemaphoreType.DMA((SLOTS,)),
            pltpu.SemaphoreType.DMA((len(writes),)),
        ],
        input_output_aliases={2 + n_env + 2 * len(parts) + k: k for k in range(len(old))},
        compiler_params=pltpu.CompilerParams(vmem_limit_bytes=VMEM_BYTES),
        cost_estimate=pl.CostEstimate(flops=flops, bytes_accessed=1, transcendentals=0),
        name="block_product",
    )(pairs, at, *environments, *(z for part in parts for z in part), *old, after)
    return results[:-1], results[-1]


def gate_kernel(*refs):
    del refs


def gate(held, after):
    out = pl.pallas_call(
        gate_kernel,
        out_shape=[jax.ShapeDtypeStruct(x.shape, x.dtype) for x in held] + [TOKEN],
        in_specs=[ANYWHERE] * (len(held) + len(after)),
        out_specs=[ANYWHERE] * (len(held) + 1),
        input_output_aliases={k: k for k in range(len(held))},
        compiler_params=pltpu.CompilerParams(vmem_limit_bytes=VMEM_BYTES),
        name="gate",
    )(*held, *after)
    return out[:-1], out[-1]


def add_kernel(count, *refs):
    pairs, outs = refs[: 2 * count], refs[2 * count + 1 : 3 * count + 1]
    held, sums, read_sem, write_sem = refs[3 * count + 2 :]
    reads = [pltpu.make_async_copy(ref, held.at[k], read_sem.at[k]) for k, ref in enumerate(pairs)]
    writes = [pltpu.make_async_copy(sums.at[k], ref, write_sem.at[k]) for k, ref in enumerate(outs)]
    for read in reads:
        read.start()
    for k, write in enumerate(writes):
        reads[2 * k].wait()
        reads[2 * k + 1].wait()
        sums[k] = (held[2 * k].astype(jnp.float32) + held[2 * k + 1].astype(jnp.float32)).astype(sums.dtype)
        write.start()
    for write in writes:
        write.wait()


def add_pairs(pairs, after, flops=1):
    count, shape = len(pairs), pairs[0][0].shape
    results = pl.pallas_call(
        functools.partial(add_kernel, count),
        out_shape=[jax.ShapeDtypeStruct(shape, jnp.bfloat16)] * count + [TOKEN],
        in_specs=[ANYWHERE] * (2 * count + 1),
        out_specs=[ANYWHERE] * (count + 1),
        scratch_shapes=[
            pltpu.VMEM((2 * count, *shape), jnp.bfloat16),
            pltpu.VMEM((count, *shape), jnp.bfloat16),
            pltpu.SemaphoreType.DMA((2 * count,)),
            pltpu.SemaphoreType.DMA((count,)),
        ],
        compiler_params=pltpu.CompilerParams(vmem_limit_bytes=VMEM_BYTES),
        cost_estimate=pl.CostEstimate(flops=flops, bytes_accessed=1, transcendentals=0),
        name="add_pairs",
    )(*(x for pair in pairs for x in pair), after)
    return results[:-1], results[-1]


def place_kernel(piece, count, flags_ref, *refs):
    pairs, out_ref = refs[: 2 * count], refs[2 * count + 2]
    held, sums, read_sem, write_sem = refs[2 * count + 4 :]
    width = pairs[0].shape[1]

    @pl.when(flags_ref[0] == 1)
    def _():
        reads = [pltpu.make_async_copy(ref, held.at[k], read_sem.at[k]) for k, ref in enumerate(pairs)]
        for read in reads:
            read.start()
        writes = []
        for k in range(count):
            reads[2 * k].wait()
            reads[2 * k + 1].wait()
            sums[k] = (held[2 * k].astype(jnp.float32) + held[2 * k + 1].astype(jnp.float32)).astype(sums.dtype)
            core = flags_ref[1] if k == 0 else 1 - flags_ref[1]
            at = pl.multiple_of(core * (out_ref.shape[1] // 2) + piece * width, LANES)
            writes.append(pltpu.make_async_copy(sums.at[k], out_ref.at[:, pl.ds(at, width)], write_sem.at[k]))
            writes[-1].start()
        for write in writes:
            write.wait()


def place(out, flags, piece, pairs, after):
    count, shape = len(pairs), pairs[0][0].shape
    return pl.pallas_call(
        functools.partial(place_kernel, piece, count),
        out_shape=[jax.ShapeDtypeStruct(out.shape, out.dtype), TOKEN],
        in_specs=[SCALARS] + [ANYWHERE] * (2 * count + 2),
        out_specs=[ANYWHERE] * 2,
        scratch_shapes=[
            pltpu.VMEM((2 * count, *shape), jnp.bfloat16),
            pltpu.VMEM((count, *shape), jnp.bfloat16),
            pltpu.SemaphoreType.DMA((2 * count,)),
            pltpu.SemaphoreType.DMA((count,)),
        ],
        input_output_aliases={1 + 2 * count: 0},
        compiler_params=pltpu.CompilerParams(vmem_limit_bytes=VMEM_BYTES),
        cost_estimate=TINY,
        name="place",
    )(flags, *(x for pair in pairs for x in pair), out, after)


def place_set_kernel(core_ref, own_ref, other_ref, old_ref, after_ref, out_ref, token_ref, held, read_sem, write_sem):
    del old_ref, after_ref, token_ref
    height, width = held.shape[1:]
    sources = (own_ref.at[pl.ds(0, height), :], other_ref)
    reads = [pltpu.make_async_copy(ref, held.at[k], read_sem.at[k]) for k, ref in enumerate(sources)]
    for read in reads:
        read.start()
    writes = []
    for k in range(2):
        reads[k].wait()
        core = core_ref[0] if k == 0 else 1 - core_ref[0]
        at = pl.multiple_of(core * (out_ref.shape[1] // 2), LANES)
        writes.append(pltpu.make_async_copy(held.at[k], out_ref.at[:, pl.ds(at, width)], write_sem.at[k]))
        writes[-1].start()
    for write in writes:
        write.wait()


def place_set(out, core, own, other, after):
    return pl.pallas_call(
        place_set_kernel,
        out_shape=[jax.ShapeDtypeStruct(out.shape, out.dtype), TOKEN],
        in_specs=[SCALARS] + [ANYWHERE] * 4,
        out_specs=[ANYWHERE] * 2,
        scratch_shapes=[
            pltpu.VMEM((2, *other.shape), other.dtype),
            pltpu.SemaphoreType.DMA((2,)),
            pltpu.SemaphoreType.DMA((2,)),
        ],
        input_output_aliases={3: 0},
        compiler_params=pltpu.CompilerParams(vmem_limit_bytes=VMEM_BYTES),
        cost_estimate=TINY,
        name="place_set",
    )(core, own, other, out, after)


def empty_kernel(out_ref):
    del out_ref


def empty(shape):
    return pl.pallas_call(
        empty_kernel,
        out_shape=jax.ShapeDtypeStruct(shape, jnp.bfloat16),
        out_specs=ANYWHERE,
        name="empty",
    )()


def line_body(n_row, n_col, sectors, environment, wavefunction):
    rows, depth = environment.shape
    planes = n_col // 2
    last = planes - 1
    ends = {0: 1, last: last - 1}

    def along_z(moves):
        return [(r * n_col + z * 2 + a, r * n_col + to * 2 + a) for r in range(n_row) for z, to in moves for a in range(2)]

    swap_pairs = along_z([(z, z ^ 1) for z in range(planes)])
    swap_middle = along_z([(1, 2), (2, 1)])
    to_ends = along_z([(1, 0), (2, 3)])
    swap_cores = [(d, d ^ 1) for d in range(n_row * n_col)]
    owners = [
        [z for z in range(planes)],
        [z ^ 1 for z in range(planes)],
        [2, 2, 1, 1],
        [3, 3, 0, 0],
    ]

    def in_plane(owner, moves):
        return [
            ((owner[z] ^ at) * n_col + z * 2 + a, (owner[z] ^ at ^ by) * n_col + z * 2 + a)
            for z in range(planes)
            for at, by in moves
            for a in range(2)
        ]

    def move(x, moves):
        return lax.ppermute(x, AXES, moves)

    row, col = lax.axis_index("row"), lax.axis_index("col")
    plane, core = col // 2, col % 2
    is_end = (plane == 0) | (plane == last)
    pairs = block_pairs(sectors, rows // BLOCK, depth // BLOCK, [col, col ^ 1])
    width = wavefunction.shape[1]
    part = width // 2
    local = [wavefunction[:, :part], wavefunction[:, part:]]
    summed = empty((n_row * 2 * rows, part))
    out = empty((rows, 2 * width))
    first, final = {}, {}
    half = [jax.ShapeDtypeStruct((rows, part), jnp.bfloat16)] * 2

    def into_set(start, tile):
        return [(start, part, 0, 2 * rows, 0, tile)]

    def into_halves(start, target):
        return [(start, part, k * rows, rows, target + k, 0) for k in range(2)]

    def product(granules, parts, old, new, writes, after):
        tiles = [jnp.asarray(owners[g])[plane] * 2 * rows for g in granules]
        at = jnp.stack([is_end, *tiles]).astype(jnp.int32)
        return block_product(pairs, at, both_rows, parts, old, new, writes, after)

    def first_step(g, made):
        ways = zip(made, (2, 1))
        first[g] = [(x, move(x, in_plane(owners[g], [(3, p), (p, p)]))) for x, p in ways]

    def second_step(g, after, flops=1):
        (own, other), token = add_pairs(first.pop(g), after, flops)
        across = [(a, b ^ 1) for a, b in in_plane(owners[g], [(2, 2)])]
        final[g] = [(own, move(own, in_plane(owners[g], [(1, 1)]))), (move(other, swap_cores), move(other, across))]
        return token

    def finish(g, out, after):
        mine = jnp.asarray(owners[g])[plane] == row
        flags = jnp.stack([mine, core]).astype(jnp.int32)
        return place(out, flags, 1, final.pop(g), after)

    nearest, middle, second, far, third = ([None, None] for _ in range(5))
    nearest[0], middle[0] = move(local[0], swap_pairs), move(local[0], swap_middle)
    nearest[1] = move(local[1], swap_pairs)
    both_rows = [environment, move(environment, swap_cores)]

    (nearest[0], middle[0]), token = gate([nearest[0], middle[0]], [pairs])
    second[0], far[0] = move(middle[0], to_ends), move(nearest[0], swap_middle)
    (nearest[1], far[0], late), token = gate([nearest[1], far[0], local[1]], [token])
    third[0], middle[1] = move(far[0], to_ends), move(late, swap_middle)

    writes = into_set(0, 1) + into_halves(part, 1)
    (summed, *made), token = product([0], [(wavefunction, wavefunction)], [summed], half, writes, token)
    first_step(0, made)
    parts = [(x, x) for x in nearest]
    (summed, *made), token = product([1], parts, [summed], half, writes, token)
    first_step(1, made)

    (second[0], middle[1]), token = gate([second[0], middle[1]], [token])
    far[1], second[1] = move(nearest[1], swap_middle), move(middle[1], to_ends)
    token = second_step(0, token)

    (third[0], far[1]), token = gate([third[0], far[1]], [token])
    third[1] = move(far[1], to_ends)
    parts = [(second[0], middle[0]), (third[0], far[0])]
    (summed,), token = product([2, 3], parts, [summed], [], into_set(0, 1) + into_set(part, 2), token)
    scattered = lax.psum_scatter(summed, "row", scatter_dimension=0, tiled=True)
    token = second_step(1, token)

    (second[1],), token = gate([second[1]], [token])
    made, token = product([], [(second[1], middle[1])], [], half, into_halves(0, 0), token)
    first_step(2, made)
    out, token = finish(0, out, token)
    out, token = finish(1, out, token)

    (third[1],), token = gate([third[1]], [token])
    made, token = product([], [(third[1], far[1])], [], half, into_halves(0, 0), token)
    first_step(3, made)
    token = second_step(2, token, HIDING)
    token = second_step(3, token)
    out, token = finish(2, out, token)
    other = move(scattered[rows:], swap_cores)
    out, token = place_set(out, core.astype(jnp.int32)[None], scattered, other, token)
    out, token = finish(3, out, token)
    return out


def gather_body(sectors, environment, wavefunction):
    rows, depth = environment.shape
    pairs = block_pairs(sectors, rows // BLOCK, depth // BLOCK, [lax.axis_index("col")])
    gathered = lax.all_gather(wavefunction, "col", axis=1, tiled=True)
    wide = gathered.shape[1]
    new, writes = jax.ShapeDtypeStruct((rows, wide), jnp.bfloat16), [(0, wide, 0, rows, 0, 0)]
    at = jnp.ones((1,), jnp.int32)
    (partial_value,), _ = block_product(pairs, at, [environment], [(gathered, gathered)], [], [new], writes, pairs)
    return lax.psum_scatter(partial_value, "row", scatter_dimension=1, tiled=True)


def solution(mesh):
    n_row, n_col = mesh.shape["row"], mesh.shape["col"]
    body = gather_body
    if n_row == 4 and n_col == 8:
        body = functools.partial(line_body, n_row, n_col)
    placed = (P(), P("col", "row"), P("row", "col"))
    return jax.shard_map(body, mesh=mesh, in_specs=placed, out_specs=P("col", "row"), check_vma=False)
```

time: 450 us -> 323 us (0.72)
  waiting for transfers between devices: 305 us -> 111 us
  Pallas kernels: 0 us -> 98.7 us
  matrix products: 90.6 us -> 0 us
  starting transfers between devices: 0.04 us -> 76.9 us
  local copies, waits for them, and re-layouts: 38.6 us -> 13.1 us
  other arithmetic: 0.08 us -> 4.75 us
    all_gather x1 -> x0, waiting for transfers between devices: 184 us -> none  [body(): gathered = lax.all_gather(wavefunction, 'col', axis=1, tiled=True)]
    reduce_scatter x1, waiting for transfers between devices: 121 us -> 0.02 us  [line_body(): scattered = lax.psum_scatter(summed, 'row', scatter_dimension=0, tiled=True)]
    ppermute x0 -> x32, waiting for transfers between devices: none -> 111 us  [move(): return lax.ppermute(x, AXES, moves)]
    pallas_call x0 -> x23, Pallas kernels: none -> 98.7 us  [the longest x5 59.5 us: block_product(): pl.pallas_call(functools.partial(product_kernel, n_env, len(parts), len(o...]
    dot_general x1 -> x0, matrix products: 90.6 us -> none  [body(): jnp.dot(masked, gathered, preferred_element_type=jnp.float32)]
    ppermute x0 -> x32, starting transfers between devices: none -> 76.9 us  [move(): return lax.ppermute(x, AXES, moves)]
    unnamed x1 -> x30, local copies, waits for them, and re-layouts: 23.6 us -> 6.15 us
    broadcast_in_dim x2 -> x0, local copies, waits for them, and re-layouts: 13.6 us -> none  [body(): allowed = jnp.repeat(jnp.repeat(allowed, BLOCK, axis=0), BLOCK, axis=1)]
  transfers between devices with their start and end apart: 2 -> 33, of which waited for: 2 -> 10; matrix products, arithmetic and copies ran while one was open for 9% -> 4% of each run, Pallas kernels for 0% -> 30%
where the time goes in v1:
time: 323 us; the launch traced here: 322 us
  waiting for transfers between devices  111 us (34%)
  Pallas kernels  98.7 us (31%)
  starting transfers between devices  76.9 us (24%)
  between operations  17.8 us (6%)
  local copies, waits for them, and re-layouts  13.1 us (4%)
  other arithmetic  4.75 us (1%)
    ppermute x32, waiting for transfers between devices, move(): return lax.ppermute(x, AXES, moves)  111 us
    ppermute x32, starting transfers between devices, move(): return lax.ppermute(x, AXES, moves)  76.9 us
    pallas_call x5, Pallas kernels, block_product(): pl.pallas_call(functools.partial(product_kernel, n_env, len(parts), len(o...  59.5 us
    pallas_call x1, Pallas kernels, block_pairs(): pl.pallas_call(functools.partial(pair_kernel, row_blocks, col_blocks), ou...  19.1 us
    pallas_call x4, Pallas kernels, add_pairs(): pl.pallas_call(functools.partial(add_kernel, count), out_shape=[jax.Shape...  11.9 us
  transfers between devices with their start and end apart: 33, of which 10 were waited for; matrix products, arithmetic and copies ran while one was open for 4% of the time, Pallas kernels for 30%

profile of v1, /device:TPU:17, one launch (start us, length us, event | category | flops | bytes accessed | tf_op | source)
XLA Modules:
  0.0 322.3 jit_solution(11767018737216630802)
XLA Ops:
  6.5 0.7 collective-permute-start
  7.2 3.8 %fusion = (bf16[6144,128]{1,0:T(8,128)(2,1)}, bf16[6144,128]{1,0:T(8,128)(2,1)}) fusion(bf16[6144,256]{1,0:T(8,128)(2,1)} %refs_3_.1), kind=kLoop, calls=%fused_computation.8 | loop fusion | bytes 6291456 | tf_op jit(solution)/shard_map/slice | solution.py:329
  11.0 1.3 collective-permute-start.2
  12.3 1.9 collective-permute-start.3
  14.9 19.1 %block_pairs.1.refs_2_.pairs_ref = s32[617]{0:T(1024)} custom-call(s32[3]{0:T(128)} %pad_add_fusion.1.bases_ref, s32[96]{0:T(128)} %sectors_ref.1), custom_call_target="tpu_custom_call" | custom-call | flops 1 | bytes 1 | tf_op jit(solution)/shard_map/block_pairs/pallas_call | solution.py:37
  34.0 13.3 %collective-permute-done.2.refs_0_ = bf16[6144,128]{1,0:T(8,128)(2,1)S(1)} collective-permute-done((bf16[6144,128]{1,0:T(8,128)(2,1)}, bf16[6144,128]{1,0:T(8,128)(2,1)S(1)}, u32[]{:S(2)}, u32[]{:S(2)}) %collective-permute-start.2) | collective-permute-done | bytes 1572896 | tf_op jit(solution)/shard_map/ppermute | solution.py:321
  47.3 2.9 collective-permute-done.3.refs_1_
  50.2 2.2 collective-permute-start.4
  52.4 2.4 collective-permute-start.9
  54.9 26.1 %collective-permute-done.1.refs_0_ = bf16[6144,128]{1,0:T(8,128)(2,1)S(1)} collective-permute-done((bf16[6144,128]{1,0:T(8,128)(2,1)}, bf16[6144,128]{1,0:T(8,128)(2,1)S(1)}, u32[]{:S(2)}, u32[]{:S(2)}) %collective-permute-start.1) | collective-permute-done | bytes 1572896 | tf_op jit(solution)/shard_map/ppermute | solution.py:321
  80.9 6.1 %collective-permute-done.4.refs_1_ = bf16[6144,128]{1,0:T(8,128)(2,1)S(1)} collective-permute-done((bf16[6144,128]{1,0:T(8,128)(2,1)}, bf16[6144,128]{1,0:T(8,128)(2,1)S(1)}, u32[]{:S(2)}, u32[]{:S(2)}) %collective-permute-start.4) | collective-permute-done | bytes 1572896 | tf_op jit(solution)/shard_map/ppermute | solution.py:321
  87.1 1.1 copy-done.6
  88.2 2.6 collective-permute-start.10
  90.8 1.4 collective-permute-start.5
  92.2 2.7 collective-permute-start.6
  95.0 0.6 copy-done.14
  95.6 0.7 dynamic_slice.26
  98.2 12.6 %block_product.5 = (bf16[24576,128]{1,0:T(8,128)(2,1)}, bf16[3072,128]{1,0:T(8,128)(2,1)}, bf16[3072,128]{1,0:T(8,128)(2,1)}, f32[8,128]{1,0:T(8,128)}) custom-call(s32[617]{0:T(1024)} %block_pairs.1.refs_2_.pairs_ref, s32[2]{0:T(128)} %pad_add_fusion.2.at_ref, bf16[3072,6144]{1,0:T(8,128)(2,1)} %refs_0_.9, ...), custom_call_target="tpu_custom_call", output_to_operand_aliasing={{0}: (6, {})} | custom-call | flops 1 | bytes 1 | tf_op jit(solution)/shard_map/block_product/pallas_call | solution.py:125
  110.7 7.5 %collective-permute-start.7 = (bf16[3072,128]{1,0:T(8,128)(2,1)}, bf16[3072,128]{1,0:T(8,128)(2,1)}, u32[]{:S(2)}, u32[]{:S(2)}) collective-permute-start(bf16[3072,128]{1,0:T(8,128)(2,1)} %get-tuple-element.64.refs_0_), channel_id=1, source_target_pairs={{24,8},{25,9},{16,0},{17,1},{18,2},{19,3},{26,10},{27,11},{12,28},... | collective-permute-start | bytes 2359304 | tf_op jit(solution)/shard_map/ppermute | solution.py:321
  118.2 1.3 collective-permute-start.8
  119.5 12.5 %block_product.6 = (bf16[24576,128]{1,0:T(8,128)(2,1)}, bf16[3072,128]{1,0:T(8,128)(2,1)}, bf16[3072,128]{1,0:T(8,128)(2,1)}, f32[8,128]{1,0:T(8,128)}) custom-call(s32[617]{0:T(1024)} %block_pairs.1.refs_2_.pairs_ref, s32[2]{0:T(128)} %pad_add_fusion.3.at_ref, bf16[3072,6144]{1,0:T(8,128)(2,1)} %refs_0_.9, ...), custom_call_target="tpu_custom_call", output_to_operand_aliasing={{0}: (8, {})} | custom-call | flops 1 | bytes 1 | tf_op jit(solution)/shard_map/block_product/pallas_call | solution.py:125
  132.1 4.3 %collective-permute-start.20 = (bf16[6144,128]{1,0:T(8,128)(2,1)}, bf16[6144,128]{1,0:T(8,128)(2,1)}, u32[]{:S(2)}, u32[]{:S(2)}) collective-permute-start(bf16[6144,128]{1,0:T(8,128)(2,1)} %get-tuple-element.85.refs_3_), channel_id=1, source_target_pairs={{2,0},{3,1},{4,6},{5,7},{10,8},{11,9},{12,14},{13,15},{18,16},{19,... | collective-permute-start | bytes 4718600 | tf_op jit(solution)/shard_map/ppermute | solution.py:321
  136.3 4.0 %collective-permute-start.12 = (bf16[3072,128]{1,0:T(8,128)(2,1)}, bf16[3072,128]{1,0:T(8,128)(2,1)}, u32[]{:S(2)}, u32[]{:S(2)}) collective-permute-start(bf16[3072,128]{1,0:T(8,128)(2,1)} %get-tuple-element.74.refs_0_), channel_id=1, source_target_pairs={{16,0},{17,1},{24,8},{25,9},{26,10},{27,11},{18,2},{19,3},{4,20},{... | collective-permute-start | bytes 2359304 | tf_op jit(solution)/shard_map/ppermute | solution.py:321
  140.4 2.2 collective-permute-start.13
  143.8 0.6 dynamic_slice.24
  145.7 3.0 add_pairs.4
  148.7 9.2 %collective-permute-done.6.refs_1_ = bf16[6144,128]{1,0:T(8,128)(2,1)S(1)} collective-permute-done((bf16[6144,128]{1,0:T(8,128)(2,1)}, bf16[6144,128]{1,0:T(8,128)(2,1)S(1)}, u32[]{:S(2)}, u32[]{:S(2)}) %collective-permute-start.6) | collective-permute-done | bytes 1572896 | tf_op jit(solution)/shard_map/ppermute | solution.py:321
  157.9 1.1 copy-done.3
  159.0 12.5 %block_product.7 = (bf16[24576,128]{1,0:T(8,128)(2,1)}, f32[8,128]{1,0:T(8,128)}) custom-call(s32[617]{0:T(1024)} %block_pairs.1.refs_2_.pairs_ref, s32[3]{0:T(128)} %pad_add_fusion.5.at_ref, bf16[3072,6144]{1,0:T(8,128)(2,1)} %refs_0_.9, bf16[3072,6144]{1,0:T(8,128)(2,1)} %collective-permute-done.refs_1_, ...), custom_call_target="tpu_custom_call", output_to_operand_aliasing={{0}: (8, {})} | custom-call | flops 1 | bytes 1 | tf_op jit(solution)/shard_map/block_product/pallas_call | solution.py:125
  171.5 1.7 collective-permute-start.17
  173.2 3.0 collective-permute-start.18
  176.2 1.4 collective-permute-start.11
  177.6 7.2 %collective-permute-start.19 = (bf16[3072,128]{1,0:T(8,128)(2,1)}, bf16[3072,128]{1,0:T(8,128)(2,1)}, u32[]{:S(2)}, u32[]{:S(2)}) collective-permute-start(bf16[3072,128]{1,0:T(8,128)(2,1)} %get-tuple-element.84), channel_id=1, source_target_pairs={{16,1},{17,0},{26,11},{27,10},{4,21},{5,20},{14,31},{15,30}} | collective-permute-start | bytes 2359304 | tf_op jit(solution)/shard_map/ppermute | solution.py:321
  184.8 3.0 add_pairs.5
  187.8 1.6 collective-permute-start.14
  189.9 1.6 collective-permute-start.16
  191.4 11.0 %block_product.8 = (bf16[3072,128]{1,0:T(8,128)(2,1)}, bf16[3072,128]{1,0:T(8,128)(2,1)}, f32[8,128]{1,0:T(8,128)}) custom-call(s32[617]{0:T(1024)} %block_pairs.1.refs_2_.pairs_ref, s32[1]{0:T(128)} %bitcast.6.at_ref, bf16[3072,6144]{1,0:T(8,128)(2,1)} %refs_0_.9, bf16[3072,6144]{1,0:T(8,128)(2,1)} %collective-permute-done.refs_1_, ...), custom_call_target="tpu_custom_call" | custom-call | flops 1 | bytes 1 | tf_op jit(solution)/shard_map/block_product/pallas_call | solution.py:125
  202.4 15.5 %collective-permute-done.19.refs_3_ = bf16[3072,128]{1,0:T(8,128)(2,1)} collective-permute-done((bf16[3072,128]{1,0:T(8,128)(2,1)}, bf16[3072,128]{1,0:T(8,128)(2,1)}, u32[]{:S(2)}, u32[]{:S(2)}) %collective-permute-start.19) | collective-permute-done | bytes 786464 | tf_op jit(solution)/shard_map/ppermute | solution.py:321
  217.9 1.3 collective-permute-start.23
  219.2 11.5 %collective-permute-start.24 = (bf16[3072,128]{1,0:T(8,128)(2,1)}, bf16[3072,128]{1,0:T(8,128)(2,1)}, u32[]{:S(2)}, u32[]{:S(2)}) collective-permute-start(bf16[3072,128]{1,0:T(8,128)(2,1)} %get-tuple-element.98.refs_2_), channel_id=1, source_target_pairs={{8,0},{9,1},{24,16},{25,17},{10,2},{11,3},{26,18},{27,19},{20,28},... | collective-permute-start | bytes 2359304 | tf_op jit(solution)/shard_map/ppermute | solution.py:321
  232.5 0.7 place.4
  233.3 0.7 place.5
  234.1 1.2 copy-done.5
  235.2 11.0 %block_product.9 = (bf16[3072,128]{1,0:T(8,128)(2,1)}, bf16[3072,128]{1,0:T(8,128)(2,1)}, f32[8,128]{1,0:T(8,128)}) custom-call(s32[617]{0:T(1024)} %block_pairs.1.refs_2_.pairs_ref, s32[1]{0:T(128)} %bitcast.6.at_ref, bf16[3072,6144]{1,0:T(8,128)(2,1)} %refs_0_.9, bf16[3072,6144]{1,0:T(8,128)(2,1)} %collective-permute-done.refs_1_, ...), custom_call_target="tpu_custom_call" | custom-call | flops 1 | bytes 1 | tf_op jit(solution)/shard_map/block_product/pallas_call | solution.py:125
  246.3 1.3 collective-permute-start.21
  247.6 1.3 collective-permute-start.22
  248.9 1.2 collective-permute-done.23.refs_1_
  250.0 3.0 add_pairs.6
  253.0 2.9 collective-permute-start.29
  256.0 2.1 collective-permute-start.30
  258.1 1.6 collective-permute-start.31
  259.7 22.5 %collective-permute-done.21.refs_1_ = bf16[3072,128]{1,0:T(8,128)(2,1)S(1)} collective-permute-done((bf16[3072,128]{1,0:T(8,128)(2,1)}, bf16[3072,128]{1,0:T(8,128)(2,1)S(1)}, u32[]{:S(2)}, u32[]{:S(2)}) %collective-permute-start.21) | collective-permute-done | bytes 786464 | tf_op jit(solution)/shard_map/ppermute | solution.py:321
  282.2 0.9 copy-done.8
  283.3 2.9 add_pairs.7
  286.3 1.3 slice.12
  287.6 0.9 collective-permute-start.28
  288.5 1.3 collective-permute-start.25
  289.9 1.3 collective-permute-start.27
  293.6 0.7 place.6
  294.4 0.9 copy-done.7
  295.3 2.3 place_set.1
  297.6 12.0 %collective-permute-done.25.refs_1_ = bf16[3072,128]{1,0:T(8,128)(2,1)} collective-permute-done((bf16[3072,128]{1,0:T(8,128)(2,1)S(1)}, bf16[3072,128]{1,0:T(8,128)(2,1)}, u32[]{:S(2)}, u32[]{:S(2)}) %collective-permute-start.25) | collective-permute-done | bytes 786464 | tf_op jit(solution)/shard_map/ppermute | solution.py:321
  309.6 2.2 collective-permute-done.27.refs_3_
  311.8 3.6 %place.7 = (bf16[3072,512]{1,0:T(8,128)(2,1)}, f32[8,128]{1,0:T(8,128)}) custom-call(s32[2]{0:T(128)} %pad_add_fusion.flags_ref, bf16[3072,128]{1,0:T(8,128)(2,1)} %get-tuple-element.101.refs_0_, bf16[3072,128]{1,0:T(8,128)(2,1)} %collective-permute-done.25.refs_1_, ...), custom_call_target="tpu_custom_call", output_to_operand_aliasing={{0}: (5, {})} | custom-call | flops 1 | bytes 1 | tf_op jit(solution)/shard_map/place/pallas_call | solution.py:225
  (69 shorter events, 6.4 us)
Async XLA Ops:
  6.5 279.8 %reduce-scatter.2.cloned.1.call-start = ((), (), s32[]{:S(2)}) async-start(), calls=%async_computation.1 | async-start | bytes 7864320 | tf_op jit(solution)/shard_map/reduce_scatter | solution.py:386
  6.5 91.6 %collective-permute-start = (bf16[3072,6144]{1,0:T(8,128)(2,1)}, bf16[3072,6144]{1,0:T(8,128)(2,1)}, u32[]{:S(2)}, u32[]{:S(2)}) collective-permute-start(bf16[3072,6144]{1,0:T(8,128)(2,1)} %refs_0_.9), channel_id=1, source_target_pairs={{0,1},{1,0},{2,3},{3,2},{4,5},{5,4},{6,7},{7,6},{8,9},{9,8},{10,11... | collective-permute-start | bytes 113246216 | tf_op jit(solution)/shard_map/ppermute | solution.py:321
  11.0 36.3 %collective-permute-start.2 = (bf16[6144,128]{1,0:T(8,128)(2,1)}, bf16[6144,128]{1,0:T(8,128)(2,1)S(1)}, u32[]{:S(2)}, u32[]{:S(2)}) collective-permute-start(bf16[6144,128]{1,0:T(8,128)(2,1)} %get-tuple-element.113), channel_id=1, source_target_pairs={{0,2},{1,3},{2,0},{3,1},{4,6},{5,7},{6,4},{7,5},{8,10},{9,11},{10,... | collective-permute-start | bytes 4718600 | tf_op jit(solution)/shard_map/ppermute | solution.py:321
  12.3 37.9 %collective-permute-start.3 = (bf16[6144,128]{1,0:T(8,128)(2,1)}, bf16[6144,128]{1,0:T(8,128)(2,1)}, u32[]{:S(2)}, u32[]{:S(2)}) collective-permute-start(bf16[6144,128]{1,0:T(8,128)(2,1)} %get-tuple-element.113), channel_id=1, source_target_pairs={{2,4},{3,5},{4,2},{5,3},{10,12},{11,13},{12,10},{13,11},{18,20},{1... | collective-permute-start | bytes 4718600 | tf_op jit(solution)/shard_map/ppermute | solution.py:321
  14.2 66.7 %collective-permute-start.1 = (bf16[6144,128]{1,0:T(8,128)(2,1)}, bf16[6144,128]{1,0:T(8,128)(2,1)S(1)}, u32[]{:S(2)}, u32[]{:S(2)}) collective-permute-start(bf16[6144,128]{1,0:T(8,128)(2,1)} %get-tuple-element.114.refs_2_), channel_id=1, source_target_pairs={{0,2},{1,3},{2,0},{3,1},{4,6},{5,7},{6,4},{7,5},{8,10},{9,11},{10,... | collective-permute-start | bytes 4718600 | tf_op jit(solution)/shard_map/ppermute | solution.py:321
  47.3 2.9 copy-start
  50.2 36.9 %collective-permute-start.4 = (bf16[6144,128]{1,0:T(8,128)(2,1)}, bf16[6144,128]{1,0:T(8,128)(2,1)S(1)}, u32[]{:S(2)}, u32[]{:S(2)}) collective-permute-start(bf16[6144,128]{1,0:T(8,128)(2,1)} %get-tuple-element.59.refs_2_.refs_3_), channel_id=1, source_target_pairs={{2,4},{3,5},{4,2},{5,3},{10,12},{11,13},{12,10},{13,11},{18,20},{1... | collective-permute-start | bytes 4718600 | tf_op jit(solution)/shard_map/ppermute | solution.py:321
  52.4 65.8 %collective-permute-start.9 = (bf16[6144,128]{1,0:T(8,128)(2,1)}, bf16[6144,128]{1,0:T(8,128)(2,1)}, u32[]{:S(2)}, u32[]{:S(2)}) collective-permute-start(bf16[6144,128]{1,0:T(8,128)(2,1)} %get-tuple-element.66.refs_3_), channel_id=1, source_target_pairs={{2,0},{3,1},{4,6},{5,7},{10,8},{11,9},{12,14},{13,15},{18,16},{19,... | collective-permute-start | bytes 4718600 | tf_op jit(solution)/shard_map/ppermute | solution.py:321
  80.9 6.1 %copy-start.1 = (bf16[6144,128]{1,0:T(8,128)(2,1)}, bf16[6144,128]{1,0:T(8,128)(2,1)S(1)}, u32[]{:S(2)}) copy-start(bf16[6144,128]{1,0:T(8,128)(2,1)S(1)} %collective-permute-done.1.refs_0_) | copy-start | bytes 4718596
  87.1 1.1 copy-start.6
  88.2 43.8 %collective-permute-start.10 = (bf16[6144,128]{1,0:T(8,128)(2,1)}, bf16[6144,128]{1,0:T(8,128)(2,1)}, u32[]{:S(2)}, u32[]{:S(2)}) collective-permute-start(bf16[6144,128]{1,0:T(8,128)(2,1)} %get-tuple-element.67), channel_id=1, source_target_pairs={{2,4},{3,5},{4,2},{5,3},{10,12},{11,13},{12,10},{13,11},{18,20},{1... | collective-permute-start | bytes 4718600 | tf_op jit(solution)/shard_map/ppermute | solution.py:321
  90.8 57.9 %collective-permute-start.5 = (bf16[6144,128]{1,0:T(8,128)(2,1)}, bf16[6144,128]{1,0:T(8,128)(2,1)S(1)}, u32[]{:S(2)}, u32[]{:S(2)}) collective-permute-start(bf16[6144,128]{1,0:T(8,128)(2,1)} %get-tuple-element.61.refs_5_), channel_id=1, source_target_pairs={{2,0},{3,1},{4,6},{5,7},{10,8},{11,9},{12,14},{13,15},{18,16},{19,... | collective-permute-start | bytes 4718600 | tf_op jit(solution)/shard_map/ppermute | solution.py:321
  92.2 65.7 %collective-permute-start.6 = (bf16[6144,128]{1,0:T(8,128)(2,1)}, bf16[6144,128]{1,0:T(8,128)(2,1)S(1)}, u32[]{:S(2)}, u32[]{:S(2)}) collective-permute-start(bf16[6144,128]{1,0:T(8,128)(2,1)} %get-tuple-element.62.refs_4_.refs_5_), channel_id=1, source_target_pairs={{2,4},{3,5},{4,2},{5,3},{10,12},{11,13},{12,10},{13,11},{18,20},{1... | collective-permute-start | bytes 4718600 | tf_op jit(solution)/shard_map/ppermute | solution.py:321
  94.9 0.7 copy-start.14
  110.7 25.6 %collective-permute-start.7 = (bf16[3072,128]{1,0:T(8,128)(2,1)}, bf16[3072,128]{1,0:T(8,128)(2,1)}, u32[]{:S(2)}, u32[]{:S(2)}) collective-permute-start(bf16[3072,128]{1,0:T(8,128)(2,1)} %get-tuple-element.64.refs_0_), channel_id=1, source_target_pairs={{24,8},{25,9},{16,0},{17,1},{18,2},{19,3},{26,10},{27,11},{12,28},... | collective-permute-start | bytes 2359304 | tf_op jit(solution)/shard_map/ppermute | solution.py:321
  118.2 22.1 %collective-permute-start.8 = (bf16[3072,128]{1,0:T(8,128)(2,1)}, bf16[3072,128]{1,0:T(8,128)(2,1)}, u32[]{:S(2)}, u32[]{:S(2)}) collective-permute-start(bf16[3072,128]{1,0:T(8,128)(2,1)} %get-tuple-element.65.refs_2_), channel_id=1, source_target_pairs={{24,16},{25,17},{8,0},{9,1},{18,26},{19,27},{2,10},{3,11},{12,4},{... | collective-permute-start | bytes 2359304 | tf_op jit(solution)/shard_map/ppermute | solution.py:321
  132.0 10.5 %copy-start.13 = (s32[4]{0:T(128)S(1)}, s32[4]{0:T(128)}, u32[]{:S(2)}) copy-start(s32[4]{0:T(128)} %constant.61.clone) | copy-start | bytes 52
  132.1 11.8 %copy-start.12 = (s32[4]{0:T(128)S(1)}, s32[4]{0:T(128)}, u32[]{:S(2)}) copy-start(s32[4]{0:T(128)} %constant.62.clone) | copy-start | bytes 52
  132.1 55.8 %collective-permute-start.20 = (bf16[6144,128]{1,0:T(8,128)(2,1)}, bf16[6144,128]{1,0:T(8,128)(2,1)}, u32[]{:S(2)}, u32[]{:S(2)}) collective-permute-start(bf16[6144,128]{1,0:T(8,128)(2,1)} %get-tuple-element.85.refs_3_), channel_id=1, source_target_pairs={{2,0},{3,1},{4,6},{5,7},{10,8},{11,9},{12,14},{13,15},{18,16},{19,... | collective-permute-start | bytes 4718600 | tf_op jit(solution)/shard_map/ppermute | solution.py:321
  136.3 39.9 %collective-permute-start.12 = (bf16[3072,128]{1,0:T(8,128)(2,1)}, bf16[3072,128]{1,0:T(8,128)(2,1)}, u32[]{:S(2)}, u32[]{:S(2)}) collective-permute-start(bf16[3072,128]{1,0:T(8,128)(2,1)} %get-tuple-element.74.refs_0_), channel_id=1, source_target_pairs={{16,0},{17,1},{24,8},{25,9},{26,10},{27,11},{18,2},{19,3},{4,20},{... | collective-permute-start | bytes 2359304 | tf_op jit(solution)/shard_map/ppermute | solution.py:321
  140.4 37.2 %collective-permute-start.13 = (bf16[3072,128]{1,0:T(8,128)(2,1)}, bf16[3072,128]{1,0:T(8,128)(2,1)}, u32[]{:S(2)}, u32[]{:S(2)}) collective-permute-start(bf16[3072,128]{1,0:T(8,128)(2,1)} %get-tuple-element.75.refs_2_), channel_id=1, source_target_pairs={{16,24},{17,25},{0,8},{1,9},{26,18},{27,19},{10,2},{11,3},{4,12},{... | collective-permute-start | bytes 2359304 | tf_op jit(solution)/shard_map/ppermute | solution.py:321
  148.7 9.2 %copy-start.2 = (bf16[6144,128]{1,0:T(8,128)(2,1)}, bf16[6144,128]{1,0:T(8,128)(2,1)S(1)}, u32[]{:S(2)}) copy-start(bf16[6144,128]{1,0:T(8,128)(2,1)S(1)} %collective-permute-done.5.refs_0_) | copy-start | bytes 4718596
  157.9 1.1 copy-start.3
  171.5 4.7 %copy-start.4 = (bf16[6144,128]{1,0:T(8,128)(2,1)S(1)}, bf16[6144,128]{1,0:T(8,128)(2,1)}, u32[]{:S(2)}) copy-start(bf16[6144,128]{1,0:T(8,128)(2,1)} %get-tuple-element.73.refs_3_) | copy-start | bytes 4718596
  171.5 17.9 %collective-permute-start.17 = (bf16[3072,128]{1,0:T(8,128)(2,1)}, bf16[3072,128]{1,0:T(8,128)(2,1)}, u32[]{:S(2)}, u32[]{:S(2)}) collective-permute-start(bf16[3072,128]{1,0:T(8,128)(2,1)} %get-tuple-element.83.refs_0_), channel_id=1, source_target_pairs={{8,0},{9,1},{2,10},{3,11},{28,20},{29,21},{22,30},{23,31}} | collective-permute-start | bytes 2359304 | tf_op jit(solution)/shard_map/ppermute | solution.py:321
  173.2 16.6 %collective-permute-start.18 = (bf16[3072,128]{1,0:T(8,128)(2,1)}, bf16[3072,128]{1,0:T(8,128)(2,1)}, u32[]{:S(2)}, u32[]{:S(2)}) collective-permute-start(bf16[3072,128]{1,0:T(8,128)(2,1)} %get-tuple-element.84), channel_id=1, source_target_pairs={{0,1},{1,0},{2,3},{3,2},{4,5},{5,4},{6,7},{7,6},{8,9},{9,8},{10,11... | collective-permute-start | bytes 2359304 | tf_op jit(solution)/shard_map/ppermute | solution.py:321
  176.2 57.8 %collective-permute-start.11 = (bf16[6144,128]{1,0:T(8,128)(2,1)S(1)}, bf16[6144,128]{1,0:T(8,128)(2,1)S(1)}, u32[]{:S(2)}, u32[]{:S(2)}) collective-permute-start(bf16[6144,128]{1,0:T(8,128)(2,1)S(1)} %copy-done.4), channel_id=1, source_target_pairs={{2,0},{3,1},{4,6},{5,7},{10,8},{11,9},{12,14},{13,15},{18,16},{19,... | collective-permute-start | bytes 4718600 | tf_op jit(solution)/shard_map/ppermute | solution.py:321
  177.6 40.3 %collective-permute-start.19 = (bf16[3072,128]{1,0:T(8,128)(2,1)}, bf16[3072,128]{1,0:T(8,128)(2,1)}, u32[]{:S(2)}, u32[]{:S(2)}) collective-permute-start(bf16[3072,128]{1,0:T(8,128)(2,1)} %get-tuple-element.84), channel_id=1, source_target_pairs={{16,1},{17,0},{26,11},{27,10},{4,21},{5,20},{14,31},{15,30}} | collective-permute-start | bytes 2359304 | tf_op jit(solution)/shard_map/ppermute | solution.py:321
  187.8 31.4 %collective-permute-start.14 = (bf16[3072,128]{1,0:T(8,128)(2,1)}, bf16[3072,128]{1,0:T(8,128)(2,1)}, u32[]{:S(2)}, u32[]{:S(2)}) collective-permute-start(bf16[3072,128]{1,0:T(8,128)(2,1)} %get-tuple-element.81.refs_0_), channel_id=1, source_target_pairs={{0,8},{1,9},{10,2},{11,3},{20,28},{21,29},{30,22},{31,23}} | collective-permute-start | bytes 2359304 | tf_op jit(solution)/shard_map/ppermute | solution.py:321
  189.4 43.9 %collective-permute-start.15 = (bf16[3072,128]{1,0:T(8,128)(2,1)}, bf16[3072,128]{1,0:T(8,128)(2,1)}, u32[]{:S(2)}, u32[]{:S(2)}) collective-permute-start(bf16[3072,128]{1,0:T(8,128)(2,1)} %get-tuple-element.82), channel_id=1, source_target_pairs={{0,1},{1,0},{2,3},{3,2},{4,5},{5,4},{6,7},{7,6},{8,9},{9,8},{10,11... | collective-permute-start | bytes 2359304 | tf_op jit(solution)/shard_map/ppermute | solution.py:321
  189.9 43.4 %collective-permute-start.16 = (bf16[3072,128]{1,0:T(8,128)(2,1)}, bf16[3072,128]{1,0:T(8,128)(2,1)}, u32[]{:S(2)}, u32[]{:S(2)}) collective-permute-start(bf16[3072,128]{1,0:T(8,128)(2,1)} %get-tuple-element.82), channel_id=1, source_target_pairs={{24,9},{25,8},{18,3},{19,2},{12,29},{13,28},{6,23},{7,22}} | collective-permute-start | bytes 2359304 | tf_op jit(solution)/shard_map/ppermute | solution.py:321
  217.9 32.1 %collective-permute-start.23 = (bf16[3072,128]{1,0:T(8,128)(2,1)}, bf16[3072,128]{1,0:T(8,128)(2,1)}, u32[]{:S(2)}, u32[]{:S(2)}) collective-permute-start(bf16[3072,128]{1,0:T(8,128)(2,1)} %get-tuple-element.97.refs_0_), channel_id=1, source_target_pairs={{8,24},{9,25},{0,16},{1,17},{10,26},{11,27},{2,18},{3,19},{20,4},{... | collective-permute-start | bytes 2359304 | tf_op jit(solution)/shard_map/ppermute | solution.py:321
  219.2 30.8 %collective-permute-start.24 = (bf16[3072,128]{1,0:T(8,128)(2,1)}, bf16[3072,128]{1,0:T(8,128)(2,1)}, u32[]{:S(2)}, u32[]{:S(2)}) collective-permute-start(bf16[3072,128]{1,0:T(8,128)(2,1)} %get-tuple-element.98.refs_2_), channel_id=1, source_target_pairs={{8,0},{9,1},{24,16},{25,17},{10,2},{11,3},{26,18},{27,19},{20,28},... | collective-permute-start | bytes 2359304 | tf_op jit(solution)/shard_map/ppermute | solution.py:321
  234.0 1.2 copy-start.5
  246.3 35.9 %collective-permute-start.21 = (bf16[3072,128]{1,0:T(8,128)(2,1)}, bf16[3072,128]{1,0:T(8,128)(2,1)S(1)}, u32[]{:S(2)}, u32[]{:S(2)}) collective-permute-start(bf16[3072,128]{1,0:T(8,128)(2,1)} %get-tuple-element.95.refs_0_), channel_id=1, source_target_pairs={{0,16},{1,17},{8,24},{9,25},{2,18},{3,19},{10,26},{11,27},{28,12},... | collective-permute-start | bytes 2359304 | tf_op jit(solution)/shard_map/ppermute | solution.py:321
  247.6 34.6 %collective-permute-start.22 = (bf16[3072,128]{1,0:T(8,128)(2,1)}, bf16[3072,128]{1,0:T(8,128)(2,1)S(1)}, u32[]{:S(2)}, u32[]{:S(2)}) collective-permute-start(bf16[3072,128]{1,0:T(8,128)(2,1)} %get-tuple-element.96.refs_2_), channel_id=1, source_target_pairs={{0,8},{1,9},{16,24},{17,25},{2,10},{3,11},{18,26},{19,27},{28,20},... | collective-permute-start | bytes 2359304 | tf_op jit(solution)/shard_map/ppermute | solution.py:321
  253.0 36.7 %collective-permute-start.29 = (bf16[3072,128]{1,0:T(8,128)(2,1)}, bf16[3072,128]{1,0:T(8,128)(2,1)S(1)}, u32[]{:S(2)}, u32[]{:S(2)}) collective-permute-start(bf16[3072,128]{1,0:T(8,128)(2,1)} %get-tuple-element.104.refs_0_), channel_id=1, source_target_pairs={{24,16},{25,17},{26,18},{27,19},{4,12},{5,13},{6,14},{7,15}} | collective-permute-start | bytes 2359304 | tf_op jit(solution)/shard_map/ppermute | solution.py:321
  256.0 33.9 %collective-permute-start.30 = (bf16[3072,128]{1,0:T(8,128)(2,1)}, bf16[3072,128]{1,0:T(8,128)(2,1)}, u32[]{:S(2)}, u32[]{:S(2)}) collective-permute-start(bf16[3072,128]{1,0:T(8,128)(2,1)} %get-tuple-element.105), channel_id=1, source_target_pairs={{0,1},{1,0},{2,3},{3,2},{4,5},{5,4},{6,7},{7,6},{8,9},{9,8},{10,11... | collective-permute-start | bytes 2359304 | tf_op jit(solution)/shard_map/ppermute | solution.py:321
  258.1 35.5 %collective-permute-start.31 = (bf16[3072,128]{1,0:T(8,128)(2,1)}, bf16[3072,128]{1,0:T(8,128)(2,1)}, u32[]{:S(2)}, u32[]{:S(2)}) collective-permute-start(bf16[3072,128]{1,0:T(8,128)(2,1)} %get-tuple-element.105), channel_id=1, source_target_pairs={{0,17},{1,16},{2,19},{3,18},{28,13},{29,12},{30,15},{31,14}} | collective-permute-start | bytes 2359304 | tf_op jit(solution)/shard_map/ppermute | solution.py:321
  282.2 0.9 copy-start.8
  282.2 1.1 copy-start.9
  286.3 2.2 copy-start.10
  287.6 6.8 %collective-permute-start.28 = (bf16[3072,128]{1,0:T(8,128)(2,1)S(1)}, bf16[3072,128]{1,0:T(8,128)(2,1)S(1)}, u32[]{:S(2)}, u32[]{:S(2)}) collective-permute-start(bf16[3072,128]{1,0:T(8,128)(2,1)S(1)} %slice.12), channel_id=1, source_target_pairs={{0,1},{1,0},{2,3},{3,2},{4,5},{5,4},{6,7},{7,6},{8,9},{9,8},{10,11... | collective-permute-start | bytes 2359304 | tf_op jit(solution)/shard_map/ppermute | solution.py:321
  288.5 21.1 %collective-permute-start.25 = (bf16[3072,128]{1,0:T(8,128)(2,1)S(1)}, bf16[3072,128]{1,0:T(8,128)(2,1)}, u32[]{:S(2)}, u32[]{:S(2)}) collective-permute-start(bf16[3072,128]{1,0:T(8,128)(2,1)S(1)} %copy-done.10), channel_id=1, source_target_pairs={{16,24},{17,25},{18,26},{19,27},{12,4},{13,5},{14,6},{15,7}} | collective-permute-start | bytes 2359304 | tf_op jit(solution)/shard_map/ppermute | solution.py:321
  289.8 3.9 %copy-start.11 = (bf16[3072,128]{1,0:T(8,128)(2,1)}, bf16[3072,128]{1,0:T(8,128)(2,1)S(1)}, u32[]{:S(2)}) copy-start(bf16[3072,128]{1,0:T(8,128)(2,1)S(1)} %collective-permute-done.29.refs_1_) | copy-start | bytes 2359300
  289.8 19.8 %collective-permute-start.26 = (bf16[3072,128]{1,0:T(8,128)(2,1)}, bf16[3072,128]{1,0:T(8,128)(2,1)}, u32[]{:S(2)}, u32[]{:S(2)}) collective-permute-start(bf16[3072,128]{1,0:T(8,128)(2,1)} %get-tuple-element.102), channel_id=1, source_target_pairs={{0,1},{1,0},{2,3},{3,2},{4,5},{5,4},{6,7},{7,6},{8,9},{9,8},{10,11... | collective-permute-start | bytes 2359304 | tf_op jit(solution)/shard_map/ppermute | solution.py:321
  289.9 21.9 %collective-permute-start.27 = (bf16[3072,128]{1,0:T(8,128)(2,1)}, bf16[3072,128]{1,0:T(8,128)(2,1)}, u32[]{:S(2)}, u32[]{:S(2)}) collective-permute-start(bf16[3072,128]{1,0:T(8,128)(2,1)} %get-tuple-element.102), channel_id=1, source_target_pairs={{8,25},{9,24},{10,27},{11,26},{20,5},{21,4},{22,7},{23,6}} | collective-permute-start | bytes 2359304 | tf_op jit(solution)/shard_map/ppermute | solution.py:321
  294.4 0.9 copy-start.7
Sparse Core Ops, SparseCore 0:
  171.7 105.2 reduce-scatter.1

commit v2 on v1

--- a/solution.py
+++ b/solution.py
@@ -11,7 +11,7 @@
 LANES = 128
 SLOTS = 32
 GROUP = 8
-HIDING = 106 * 10**9
+HIDING = 115 * 10**9
 AXES = ("row", "col")
 VMEM_BYTES = 60 * 1024 * 1024
 TINY = pl.CostEstimate(flops=1, bytes_accessed=1, transcendentals=0)
@@ -161,34 +161,41 @@
     return out[:-1], out[-1]
 
 
-def add_kernel(count, *refs):
-    pairs, outs = refs[: 2 * count], refs[2 * count + 1 : 3 * count + 1]
-    held, sums, read_sem, write_sem = refs[3 * count + 2 :]
-    reads = [pltpu.make_async_copy(ref, held.at[k], read_sem.at[k]) for k, ref in enumerate(pairs)]
-    writes = [pltpu.make_async_copy(sums.at[k], ref, write_sem.at[k]) for k, ref in enumerate(outs)]
-    for read in reads:
-        read.start()
+def add_kernel(count, parts, *refs):
+    pairs, outs = refs[: 2 * count], refs[2 * count + 1 : (2 + parts) * count + 1]
+    held, sums, read_sem, write_sem = refs[(2 + parts) * count + 2 :]
+    high = sums.shape[1] // parts
+    reads, writes = [], []
+    for k in range(count * parts):
+        rows = pl.ds(k % parts * high, high)
+        for n in range(2):
+            at = k // parts * 2 + n
+            reads.append(pltpu.make_async_copy(pairs[at].at[rows, :], held.at[at, rows, :], read_sem.at[2 * k + n]))
+            reads[-1].start()
+        writes.append(pltpu.make_async_copy(sums.at[k // parts, rows, :], outs[k], write_sem.at[k]))
     for k, write in enumerate(writes):
         reads[2 * k].wait()
         reads[2 * k + 1].wait()
-        sums[k] = (held[2 * k].astype(jnp.float32) + held[2 * k + 1].astype(jnp.float32)).astype(sums.dtype)
+        rows, at = pl.ds(k % parts * high, high), k // parts
+        both = held[2 * at, rows, :].astype(jnp.float32) + held[2 * at + 1, rows, :].astype(jnp.float32)
+        sums[at, rows, :] = both.astype(sums.dtype)
         write.start()
     for write in writes:
         write.wait()
 
 
-def add_pairs(pairs, after, flops=1):
+def add_pairs(pairs, after, flops=1, parts=1):
     count, shape = len(pairs), pairs[0][0].shape
     results = pl.pallas_call(
-        functools.partial(add_kernel, count),
-        out_shape=[jax.ShapeDtypeStruct(shape, jnp.bfloat16)] * count + [TOKEN],
+        functools.partial(add_kernel, count, parts),
+        out_shape=[jax.ShapeDtypeStruct((shape[0] // parts, shape[1]), jnp.bfloat16)] * (count * parts) + [TOKEN],
         in_specs=[ANYWHERE] * (2 * count + 1),
-        out_specs=[ANYWHERE] * (count + 1),
+        out_specs=[ANYWHERE] * (count * parts + 1),
         scratch_shapes=[
             pltpu.VMEM((2 * count, *shape), jnp.bfloat16),
             pltpu.VMEM((count, *shape), jnp.bfloat16),
-            pltpu.SemaphoreType.DMA((2 * count,)),
-            pltpu.SemaphoreType.DMA((count,)),
+            pltpu.SemaphoreType.DMA((2 * count * parts,)),
+            pltpu.SemaphoreType.DMA((count * parts,)),
         ],
         compiler_params=pltpu.CompilerParams(vmem_limit_bytes=VMEM_BYTES),
         cost_estimate=pl.CostEstimate(flops=flops, bytes_accessed=1, transcendentals=0),
@@ -240,27 +247,30 @@
     )(flags, *(x for pair in pairs for x in pair), out, after)
 
 
-def place_set_kernel(core_ref, own_ref, other_ref, old_ref, after_ref, out_ref, token_ref, held, read_sem, write_sem):
+def place_set_kernel(piece, flags_ref, own_ref, other_ref, old_ref, after_ref, out_ref, token_ref, held, read_sem, write_sem):
     del old_ref, after_ref, token_ref
     height, width = held.shape[1:]
-    sources = (own_ref.at[pl.ds(0, height), :], other_ref)
-    reads = [pltpu.make_async_copy(ref, held.at[k], read_sem.at[k]) for k, ref in enumerate(sources)]
-    for read in reads:
-        read.start()
-    writes = []
-    for k in range(2):
-        reads[k].wait()
-        core = core_ref[0] if k == 0 else 1 - core_ref[0]
-        at = pl.multiple_of(core * (out_ref.shape[1] // 2), LANES)
-        writes.append(pltpu.make_async_copy(held.at[k], out_ref.at[:, pl.ds(at, width)], write_sem.at[k]))
-        writes[-1].start()
-    for write in writes:
-        write.wait()
-
-
-def place_set(out, core, own, other, after):
+
+    @pl.when(flags_ref[0] == 1)
+    def _():
+        sources = (own_ref.at[pl.ds(0, height), :], other_ref)
+        reads = [pltpu.make_async_copy(ref, held.at[k], read_sem.at[k]) for k, ref in enumerate(sources)]
+        for read in reads:
+            read.start()
+        writes = []
+        for k in range(2):
+            reads[k].wait()
+            core = flags_ref[1] if k == 0 else 1 - flags_ref[1]
+            at = pl.multiple_of(core * (out_ref.shape[1] // 2) + piece * width, LANES)
+            writes.append(pltpu.make_async_copy(held.at[k], out_ref.at[:, pl.ds(at, width)], write_sem.at[k]))
+            writes[-1].start()
+        for write in writes:
+            write.wait()
+
+
+def place_set(out, flags, piece, own, other, after):
     return pl.pallas_call(
-        place_set_kernel,
+        functools.partial(place_set_kernel, piece),
         out_shape=[jax.ShapeDtypeStruct(out.shape, out.dtype), TOKEN],
         in_specs=[SCALARS] + [ANYWHERE] * 4,
         out_specs=[ANYWHERE] * 2,
@@ -273,7 +283,7 @@
         compiler_params=pltpu.CompilerParams(vmem_limit_bytes=VMEM_BYTES),
         cost_estimate=TINY,
         name="place_set",
-    )(core, own, other, out, after)
+    )(flags, own, other, out, after)
 
 
 def empty_kernel(out_ref):
@@ -353,10 +363,28 @@
         final[g] = [(own, move(own, in_plane(owners[g], [(1, 1)]))), (move(other, swap_cores), move(other, across))]
         return token
 
+    def first_whole(g, made, p):
+        first[g] = made, move(made, in_plane(owners[g], [(3, p), (p, p)]))
+
+    def second_whole(g, q, after):
+        (made,), token = add_pairs([first.pop(g)], after)
+        final[g] = made, move(made, in_plane(owners[g], [(q, q)]))
+        return token
+
+    def add_whole(g, after):
+        (own, other), token = add_pairs([final.pop(g)], after, 1, 2)
+        final[g] = own, move(other, swap_cores)
+        return token
+
+    def flags(g):
+        mine = jnp.asarray(owners[g])[plane] == row
+        return jnp.stack([mine, core]).astype(jnp.int32)
+
+    def finish_whole(g, out, after):
+        return place_set(out, flags(g), 1, *final.pop(g), after)
+
     def finish(g, out, after):
-        mine = jnp.asarray(owners[g])[plane] == row
-        flags = jnp.stack([mine, core]).astype(jnp.int32)
-        return place(out, flags, 1, final.pop(g), after)
+        return place(out, flags(g), 1, final.pop(g), after)
 
     nearest, middle, second, far, third = ([None, None] for _ in range(5))
     nearest[0], middle[0] = move(local[0], swap_pairs), move(local[0], swap_middle)
@@ -368,38 +396,41 @@
     (nearest[1], far[0], late), token = gate([nearest[1], far[0], local[1]], [token])
     third[0], middle[1] = move(far[0], to_ends), move(late, swap_middle)
 
-    writes = into_set(0, 1) + into_halves(part, 1)
-    (summed, *made), token = product([0], [(wavefunction, wavefunction)], [summed], half, writes, token)
-    first_step(0, made)
-    parts = [(x, x) for x in nearest]
-    (summed, *made), token = product([1], parts, [summed], half, writes, token)
-    first_step(1, made)
+    whole = [jax.ShapeDtypeStruct((2 * rows, part), jnp.bfloat16)]
+    writes = into_set(0, 1) + [(part, part, 0, 2 * rows, 1, 0)]
+    (summed, made), token = product([0], [(wavefunction, wavefunction)], [summed], whole, writes, token)
+    first_whole(0, made, 2)
+    (summed, made), token = product([1], [(x, x) for x in nearest], [summed], whole, writes, token)
+    first_whole(1, made, 1)
 
     (second[0], middle[1]), token = gate([second[0], middle[1]], [token])
     far[1], second[1] = move(nearest[1], swap_middle), move(middle[1], to_ends)
-    token = second_step(0, token)
+    token = second_whole(0, 1, token)
 
     (third[0], far[1]), token = gate([third[0], far[1]], [token])
     third[1] = move(far[1], to_ends)
     parts = [(second[0], middle[0]), (third[0], far[0])]
     (summed,), token = product([2, 3], parts, [summed], [], into_set(0, 1) + into_set(part, 2), token)
     scattered = lax.psum_scatter(summed, "row", scatter_dimension=0, tiled=True)
-    token = second_step(1, token)
+    token = second_whole(1, 2, token)
 
     (second[1],), token = gate([second[1]], [token])
     made, token = product([], [(second[1], middle[1])], [], half, into_halves(0, 0), token)
     first_step(2, made)
-    out, token = finish(0, out, token)
-    out, token = finish(1, out, token)
+    token = add_whole(0, token)
 
     (third[1],), token = gate([third[1]], [token])
     made, token = product([], [(third[1], far[1])], [], half, into_halves(0, 0), token)
     first_step(3, made)
     token = second_step(2, token, HIDING)
+    token = add_whole(1, token)
+    out, token = finish_whole(0, out, token)
     token = second_step(3, token)
+    out, token = finish_whole(1, out, token)
     out, token = finish(2, out, token)
     other = move(scattered[rows:], swap_cores)
-    out, token = place_set(out, core.astype(jnp.int32)[None], scattered, other, token)
+    everywhere = jnp.stack([jnp.ones_like(core), core]).astype(jnp.int32)
+    out, token = place_set(out, everywhere, 0, scattered, other, token)
     out, token = finish(3, out, token)
     return out
 

time: 323 us -> 316 us (0.978)
  Pallas kernels: 98.7 us -> 111 us
  starting transfers between devices: 76.9 us -> 65.6 us
  waiting for transfers between devices: 111 us -> 101 us
    ppermute x32 -> x28, waiting for transfers between devices: 111 us -> 97.9 us  [move(): return lax.ppermute(x, AXES, moves)]
    ppermute x32 -> x28, starting transfers between devices: 76.9 us -> 65.6 us  [move(): return lax.ppermute(x, AXES, moves)]
    pallas_call x5 -> x9, Pallas kernels: 14.2 us -> 23.2 us  [the longest x6 18.8 us: add_pairs(): pl.pallas_call(functools.partial(add_kernel, count, parts), out_shape=[ja...]
    pallas_call x5, Pallas kernels: 59.5 us -> 64.4 us  [block_product(): pl.pallas_call(functools.partial(product_kernel, n_env, len(parts), len(o...]
  transfers between devices with their start and end apart: 33 -> 29, of which waited for: 10 -> 14; matrix products, arithmetic and copies ran while one was open for 4% -> 4% of each run, Pallas kernels for 30% -> 34%
where the time goes in v2:
time: 316 us; the launch traced here: 313 us
  Pallas kernels  111 us (35%)
  waiting for transfers between devices  101 us (32%)
  starting transfers between devices  65.6 us (21%)
  between operations  17.5 us (6%)
  local copies, waits for them, and re-layouts  12 us (4%)
  other arithmetic  5.6 us (2%)
    ppermute x28, waiting for transfers between devices, move(): return lax.ppermute(x, AXES, moves)  97.9 us
    ppermute x28, starting transfers between devices, move(): return lax.ppermute(x, AXES, moves)  65.6 us
    pallas_call x5, Pallas kernels, block_product(): pl.pallas_call(functools.partial(product_kernel, n_env, len(parts), len(o...  64.4 us
    pallas_call x1, Pallas kernels, block_pairs(): pl.pallas_call(functools.partial(pair_kernel, row_blocks, col_blocks), ou...  19.1 us
    pallas_call x6, Pallas kernels, add_pairs(): pl.pallas_call(functools.partial(add_kernel, count, parts), out_shape=[ja...  18.8 us
  transfers between devices with their start and end apart: 29, of which 14 were waited for; matrix products, arithmetic and copies ran while one was open for 4% of the time, Pallas kernels for 34%

profile of v2, /device:TPU:17, one launch (start us, length us, event | category | flops | bytes accessed | tf_op | source)
XLA Modules:
  0.0 312.9 jit_solution(7617097053932555484)
XLA Ops:
  6.5 0.7 collective-permute-start
  7.2 3.8 %fusion = (bf16[6144,128]{1,0:T(8,128)(2,1)}, bf16[6144,128]{1,0:T(8,128)(2,1)}) fusion(bf16[6144,256]{1,0:T(8,128)(2,1)} %refs_3_.1), kind=kLoop, calls=%fused_computation.9 | loop fusion | bytes 6291456 | tf_op jit(solution)/shard_map/slice | solution.py:339
  11.0 1.3 collective-permute-start.2
  12.3 1.9 collective-permute-start.3
  14.9 19.1 %block_pairs.1.refs_2_.pairs_ref = s32[617]{0:T(1024)} custom-call(s32[3]{0:T(128)} %pad_add_fusion.1.bases_ref, s32[96]{0:T(128)} %sectors_ref.1), custom_call_target="tpu_custom_call" | custom-call | flops 1 | bytes 1 | tf_op jit(solution)/shard_map/block_pairs/pallas_call | solution.py:37
  34.1 13.3 %collective-permute-done.2.refs_0_ = bf16[6144,128]{1,0:T(8,128)(2,1)S(1)} collective-permute-done((bf16[6144,128]{1,0:T(8,128)(2,1)}, bf16[6144,128]{1,0:T(8,128)(2,1)S(1)}, u32[]{:S(2)}, u32[]{:S(2)}) %collective-permute-start.2) | collective-permute-done | bytes 1572896 | tf_op jit(solution)/shard_map/ppermute | solution.py:331
  47.3 2.9 collective-permute-done.3.refs_1_
  50.2 2.2 collective-permute-start.4
  52.4 2.4 collective-permute-start.8
  54.9 26.2 %collective-permute-done.1.refs_0_ = bf16[6144,128]{1,0:T(8,128)(2,1)S(1)} collective-permute-done((bf16[6144,128]{1,0:T(8,128)(2,1)}, bf16[6144,128]{1,0:T(8,128)(2,1)S(1)}, u32[]{:S(2)}, u32[]{:S(2)}) %collective-permute-start.1) | collective-permute-done | bytes 1572896 | tf_op jit(solution)/shard_map/ppermute | solution.py:331
  81.0 6.1 %collective-permute-done.4.refs_1_ = bf16[6144,128]{1,0:T(8,128)(2,1)} collective-permute-done((bf16[6144,128]{1,0:T(8,128)(2,1)}, bf16[6144,128]{1,0:T(8,128)(2,1)}, u32[]{:S(2)}, u32[]{:S(2)}) %collective-permute-start.4) | collective-permute-done | bytes 1572896 | tf_op jit(solution)/shard_map/ppermute | solution.py:331
  87.2 2.6 collective-permute-start.9
  90.4 13.4 %block_product.5 = (bf16[24576,128]{1,0:T(8,128)(2,1)}, bf16[6144,128]{1,0:T(8,128)(2,1)}, f32[8,128]{1,0:T(8,128)}) custom-call(s32[617]{0:T(1024)} %block_pairs.1.refs_2_.pairs_ref, s32[2]{0:T(128)} %pad_add_fusion.2.at_ref, bf16[3072,6144]{1,0:T(8,128)(2,1)} %refs_0_.9, ...), custom_call_target="tpu_custom_call", output_to_operand_aliasing={{0}: (6, {})} | custom-call | flops 1 | bytes 1 | tf_op jit(solution)/shard_map/block_product/pallas_call | solution.py:125
  103.8 5.0 %collective-permute-start.7 = (bf16[6144,128]{1,0:T(8,128)(2,1)}, bf16[6144,128]{1,0:T(8,128)(2,1)}, u32[]{:S(2)}, u32[]{:S(2)}) collective-permute-start(bf16[6144,128]{1,0:T(8,128)(2,1)} %get-tuple-element.66.refs_0_), channel_id=1, source_target_pairs={{24,8},{25,9},{16,0},{17,1},{18,2},{19,3},{26,10},{27,11},{12,28},... | collective-permute-start | bytes 4718600 | tf_op jit(solution)/shard_map/ppermute | solution.py:331
  108.8 2.4 collective-permute-start.5
  111.2 1.9 collective-permute-start.6
  115.0 13.3 %block_product.6 = (bf16[24576,128]{1,0:T(8,128)(2,1)}, bf16[6144,128]{1,0:T(8,128)(2,1)}, f32[8,128]{1,0:T(8,128)}) custom-call(s32[617]{0:T(1024)} %block_pairs.1.refs_2_.pairs_ref, s32[2]{0:T(128)} %pad_add_fusion.3.at_ref, bf16[3072,6144]{1,0:T(8,128)(2,1)} %refs_0_.9, ...), custom_call_target="tpu_custom_call", output_to_operand_aliasing={{0}: (8, {})} | custom-call | flops 1 | bytes 1 | tf_op jit(solution)/shard_map/block_product/pallas_call | solution.py:125
  128.3 2.5 collective-permute-start.13
  130.8 1.1 copy-done.3
  131.9 1.4 collective-permute-start.12
  133.3 6.3 %collective-permute-done.7.refs_1_ = bf16[6144,128]{1,0:T(8,128)(2,1)} collective-permute-done((bf16[6144,128]{1,0:T(8,128)(2,1)}, bf16[6144,128]{1,0:T(8,128)(2,1)}, u32[]{:S(2)}, u32[]{:S(2)}) %collective-permute-start.7) | collective-permute-done | bytes 1572896 | tf_op jit(solution)/shard_map/ppermute | solution.py:331
  139.7 3.4 %add_pairs.6 = (bf16[6144,128]{1,0:T(8,128)(2,1)}, f32[8,128]{1,0:T(8,128)}) custom-call(bf16[6144,128]{1,0:T(8,128)(2,1)} %get-tuple-element.66.refs_0_, bf16[6144,128]{1,0:T(8,128)(2,1)} %collective-permute-done.7.refs_1_, f32[8,128]{1,0:T(8,128)} %get-tuple-element.72.refs_2_), custom_call_target="tpu_custom_call" | custom-call | flops 1 | bytes 1 | tf_op jit(solution)/shard_map/add_pairs/pallas_call | solution.py:189
  143.1 1.8 collective-permute-start.11
  144.9 2.6 collective-permute-done.5.refs_0_
  147.5 9.4 %collective-permute-done.6.refs_1_ = bf16[6144,128]{1,0:T(8,128)(2,1)} collective-permute-done((bf16[6144,128]{1,0:T(8,128)(2,1)S(1)}, bf16[6144,128]{1,0:T(8,128)(2,1)}, u32[]{:S(2)}, u32[]{:S(2)}) %collective-permute-start.6) | collective-permute-done | bytes 1572896 | tf_op jit(solution)/shard_map/ppermute | solution.py:331
  157.0 1.5 collective-permute-start.10
  160.9 0.7 pad_add_fusion.4.at_ref
  161.6 13.2 %block_product.7 = (bf16[24576,128]{1,0:T(8,128)(2,1)}, f32[8,128]{1,0:T(8,128)}) custom-call(s32[617]{0:T(1024)} %block_pairs.1.refs_2_.pairs_ref, s32[3]{0:T(128)} %pad_add_fusion.4.at_ref, bf16[3072,6144]{1,0:T(8,128)(2,1)} %refs_0_.9, bf16[3072,6144]{1,0:T(8,128)(2,1)} %collective-permute-done.refs_1_, ...), custom_call_target="tpu_custom_call", output_to_operand_aliasing={{0}: (8, {})} | custom-call | flops 1 | bytes 1 | tf_op jit(solution)/shard_map/block_product/pallas_call | solution.py:125
  174.8 3.4 %add_pairs.7 = (bf16[6144,128]{1,0:T(8,128)(2,1)}, f32[8,128]{1,0:T(8,128)}) custom-call(bf16[6144,128]{1,0:T(8,128)(2,1)} %get-tuple-element.77.refs_0_, bf16[6144,128]{1,0:T(8,128)(2,1)} %collective-permute-done.13.refs_1_, f32[8,128]{1,0:T(8,128)} %get-tuple-element.82.refs_2_), custom_call_target="tpu_custom_call" | custom-call | flops 1 | bytes 1 | tf_op jit(solution)/shard_map/add_pairs/pallas_call | solution.py:189
  178.2 3.0 collective-permute-done.12.refs_0_
  181.3 1.1 copy-done.5
  182.4 12.9 %block_product.8 = (bf16[3072,128]{1,0:T(8,128)(2,1)}, bf16[3072,128]{1,0:T(8,128)(2,1)}, f32[8,128]{1,0:T(8,128)}) custom-call(s32[617]{0:T(1024)} %block_pairs.1.refs_2_.pairs_ref, s32[1]{0:T(128)} %bitcast.6.at_ref, bf16[3072,6144]{1,0:T(8,128)(2,1)} %refs_0_.9, bf16[3072,6144]{1,0:T(8,128)(2,1)} %collective-permute-done.refs_1_, ...), custom_call_target="tpu_custom_call" | custom-call | flops 1 | bytes 1 | tf_op jit(solution)/shard_map/block_product/pallas_call | solution.py:125
  195.3 1.3 collective-permute-start.18
  196.6 2.7 collective-permute-start.19
  199.3 1.8 collective-permute-start.17
  201.1 3.0 add_pairs.8
  204.1 1.2 collective-permute-start.16
  205.3 9.7 %collective-permute-done.10.refs_0_ = bf16[6144,128]{1,0:T(8,128)(2,1)S(1)} collective-permute-done((bf16[6144,128]{1,0:T(8,128)(2,1)}, bf16[6144,128]{1,0:T(8,128)(2,1)S(1)}, u32[]{:S(2)}, u32[]{:S(2)}) %collective-permute-start.10) | collective-permute-done | bytes 1572896 | tf_op jit(solution)/shard_map/ppermute | solution.py:331
  215.0 1.1 copy-done.4
  216.1 11.7 %block_product.9 = (bf16[3072,128]{1,0:T(8,128)(2,1)}, bf16[3072,128]{1,0:T(8,128)(2,1)}, f32[8,128]{1,0:T(8,128)}) custom-call(s32[617]{0:T(1024)} %block_pairs.1.refs_2_.pairs_ref, s32[1]{0:T(128)} %bitcast.6.at_ref, bf16[3072,6144]{1,0:T(8,128)(2,1)} %refs_0_.9, bf16[3072,6144]{1,0:T(8,128)(2,1)} %collective-permute-done.refs_1_, ...), custom_call_target="tpu_custom_call" | custom-call | flops 1 | bytes 1 | tf_op jit(solution)/shard_map/block_product/pallas_call | solution.py:125
  227.8 1.3 collective-permute-start.14
  229.1 4.3 %collective-permute-done.18.refs_1_ = bf16[3072,128]{1,0:T(8,128)(2,1)} collective-permute-done((bf16[3072,128]{1,0:T(8,128)(2,1)}, bf16[3072,128]{1,0:T(8,128)(2,1)}, u32[]{:S(2)}, u32[]{:S(2)}) %collective-permute-start.18) | collective-permute-done | bytes 786464 | tf_op jit(solution)/shard_map/ppermute | solution.py:331
  233.5 1.5 collective-permute-start.15
  235.0 3.0 add_pairs.9
  238.0 3.1 add_pairs.10
  241.0 2.2 collective-permute-start.27
  243.2 20.1 %collective-permute-start.24 = (bf16[3072,128]{1,0:T(8,128)(2,1)S(1)}, bf16[3072,128]{1,0:T(8,128)(2,1)S(1)}, u32[]{:S(2)}, u32[]{:S(2)}) collective-permute-start(bf16[3072,128]{1,0:T(8,128)(2,1)S(1)} %copy-done.10), channel_id=1, source_target_pairs={{24,16},{25,17},{26,18},{27,19},{4,12},{5,13},{6,14},{7,15}} | collective-permute-start | bytes 2359304 | tf_op jit(solution)/shard_map/ppermute | solution.py:331
  264.4 0.7 place_set.3
  265.1 1.5 collective-permute-start.26
  266.7 0.9 copy-done.9
  267.6 3.0 add_pairs.11
  270.6 3.1 reduce-scatter.2.cloned.1.call-done.own_ref
  273.7 1.2 slice.12
  275.4 1.3 collective-permute-start.20
  276.7 3.6 %collective-permute-done.24.refs_1_ = bf16[3072,128]{1,0:T(8,128)(2,1)S(1)} collective-permute-done((bf16[3072,128]{1,0:T(8,128)(2,1)S(1)}, bf16[3072,128]{1,0:T(8,128)(2,1)S(1)}, u32[]{:S(2)}, u32[]{:S(2)}) %collective-permute-start.24) | collective-permute-done | bytes 786464 | tf_op jit(solution)/shard_map/ppermute | solution.py:331
  280.2 0.8 collective-permute-start.21
  281.0 1.3 collective-permute-start.22
  286.6 0.7 place_set.4
  287.3 0.7 place.2
  288.1 0.9 copy-done.7
  289.0 3.0 place_set.5
  292.0 4.7 %collective-permute-done.20.refs_1_ = bf16[3072,128]{1,0:T(8,128)(2,1)} collective-permute-done((bf16[3072,128]{1,0:T(8,128)(2,1)}, bf16[3072,128]{1,0:T(8,128)(2,1)}, u32[]{:S(2)}, u32[]{:S(2)}) %collective-permute-start.20) | collective-permute-done | bytes 786464 | tf_op jit(solution)/shard_map/ppermute | solution.py:331
  296.7 5.7 %collective-permute-done.22.refs_3_ = bf16[3072,128]{1,0:T(8,128)(2,1)} collective-permute-done((bf16[3072,128]{1,0:T(8,128)(2,1)}, bf16[3072,128]{1,0:T(8,128)(2,1)}, u32[]{:S(2)}, u32[]{:S(2)}) %collective-permute-start.22) | collective-permute-done | bytes 786464 | tf_op jit(solution)/shard_map/ppermute | solution.py:331
  302.4 3.6 %place.3 = (bf16[3072,512]{1,0:T(8,128)(2,1)}, f32[8,128]{1,0:T(8,128)}) custom-call(s32[2]{0:T(128)} %pad_add_fusion.flags_ref, bf16[3072,128]{1,0:T(8,128)(2,1)} %get-tuple-element.101.refs_0_, bf16[3072,128]{1,0:T(8,128)(2,1)} %collective-permute-done.20.refs_1_, bf16[3072,128]{1,0:T(8,128)(2,1)} %copy-done.12, ...), custom_call_target="tpu_custom_call", output_to_operand_aliasing={{0}: (5, {})} | custom-call | flops 1 | bytes 1 | tf_op jit(solution)/shard_map/place/pallas_call | solution.py:232
  (66 shorter events, 7.9 us)
Async XLA Ops:
  6.5 267.1 %reduce-scatter.2.cloned.1.call-start = ((), (), s32[]{:S(2)}) async-start(), calls=%async_computation.1 | async-start | bytes 7864320 | tf_op jit(solution)/shard_map/reduce_scatter | solution.py:414
  6.5 83.9 %collective-permute-start = (bf16[3072,6144]{1,0:T(8,128)(2,1)}, bf16[3072,6144]{1,0:T(8,128)(2,1)}, u32[]{:S(2)}, u32[]{:S(2)}) collective-permute-start(bf16[3072,6144]{1,0:T(8,128)(2,1)} %refs_0_.9), channel_id=1, source_target_pairs={{0,1},{1,0},{2,3},{3,2},{4,5},{5,4},{6,7},{7,6},{8,9},{9,8},{10,11... | collective-permute-start | bytes 113246216 | tf_op jit(solution)/shard_map/ppermute | solution.py:331
  11.0 36.3 %collective-permute-start.2 = (bf16[6144,128]{1,0:T(8,128)(2,1)}, bf16[6144,128]{1,0:T(8,128)(2,1)S(1)}, u32[]{:S(2)}, u32[]{:S(2)}) collective-permute-start(bf16[6144,128]{1,0:T(8,128)(2,1)} %get-tuple-element.117), channel_id=1, source_target_pairs={{0,2},{1,3},{2,0},{3,1},{4,6},{5,7},{6,4},{7,5},{8,10},{9,11},{10,... | collective-permute-start | bytes 4718600 | tf_op jit(solution)/shard_map/ppermute | solution.py:331
  12.3 37.9 %collective-permute-start.3 = (bf16[6144,128]{1,0:T(8,128)(2,1)}, bf16[6144,128]{1,0:T(8,128)(2,1)}, u32[]{:S(2)}, u32[]{:S(2)}) collective-permute-start(bf16[6144,128]{1,0:T(8,128)(2,1)} %get-tuple-element.117), channel_id=1, source_target_pairs={{2,4},{3,5},{4,2},{5,3},{10,12},{11,13},{12,10},{13,11},{18,20},{1... | collective-permute-start | bytes 4718600 | tf_op jit(solution)/shard_map/ppermute | solution.py:331
  14.2 66.8 %collective-permute-start.1 = (bf16[6144,128]{1,0:T(8,128)(2,1)}, bf16[6144,128]{1,0:T(8,128)(2,1)S(1)}, u32[]{:S(2)}, u32[]{:S(2)}) collective-permute-start(bf16[6144,128]{1,0:T(8,128)(2,1)} %get-tuple-element.118.refs_2_), channel_id=1, source_target_pairs={{0,2},{1,3},{2,0},{3,1},{4,6},{5,7},{6,4},{7,5},{8,10},{9,11},{10,... | collective-permute-start | bytes 4718600 | tf_op jit(solution)/shard_map/ppermute | solution.py:331
  47.3 2.9 copy-start
  50.2 37.0 %collective-permute-start.4 = (bf16[6144,128]{1,0:T(8,128)(2,1)}, bf16[6144,128]{1,0:T(8,128)(2,1)}, u32[]{:S(2)}, u32[]{:S(2)}) collective-permute-start(bf16[6144,128]{1,0:T(8,128)(2,1)} %get-tuple-element.61.refs_2_.refs_3_), channel_id=1, source_target_pairs={{2,4},{3,5},{4,2},{5,3},{10,12},{11,13},{12,10},{13,11},{18,20},{1... | collective-permute-start | bytes 4718600 | tf_op jit(solution)/shard_map/ppermute | solution.py:331
  52.4 75.9 %collective-permute-start.8 = (bf16[6144,128]{1,0:T(8,128)(2,1)}, bf16[6144,128]{1,0:T(8,128)(2,1)}, u32[]{:S(2)}, u32[]{:S(2)}) collective-permute-start(bf16[6144,128]{1,0:T(8,128)(2,1)} %get-tuple-element.67.refs_3_), channel_id=1, source_target_pairs={{2,0},{3,1},{4,6},{5,7},{10,8},{11,9},{12,14},{13,15},{18,16},{19,... | collective-permute-start | bytes 4718600 | tf_op jit(solution)/shard_map/ppermute | solution.py:331
  81.0 6.1 %copy-start.1 = (bf16[6144,128]{1,0:T(8,128)(2,1)}, bf16[6144,128]{1,0:T(8,128)(2,1)S(1)}, u32[]{:S(2)}) copy-start(bf16[6144,128]{1,0:T(8,128)(2,1)S(1)} %collective-permute-done.1.refs_0_) | copy-start | bytes 4718596
  87.2 43.6 %collective-permute-start.9 = (bf16[6144,128]{1,0:T(8,128)(2,1)}, bf16[6144,128]{1,0:T(8,128)(2,1)S(1)}, u32[]{:S(2)}, u32[]{:S(2)}) collective-permute-start(bf16[6144,128]{1,0:T(8,128)(2,1)} %get-tuple-element.68), channel_id=1, source_target_pairs={{2,4},{3,5},{4,2},{5,3},{10,12},{11,13},{12,10},{13,11},{18,20},{1... | collective-permute-start | bytes 4718600 | tf_op jit(solution)/shard_map/ppermute | solution.py:331
  90.4 20.8 %copy-start.2 = (bf16[6144,128]{1,0:T(8,128)(2,1)S(1)}, bf16[6144,128]{1,0:T(8,128)(2,1)}, u32[]{:S(2)}) copy-start(bf16[6144,128]{1,0:T(8,128)(2,1)} %get-tuple-element.64.refs_4_.refs_5_) | copy-start | bytes 4718596
  90.4 22.7 %copy-start.15 = (s32[4]{0:T(128)S(1)}, s32[4]{0:T(128)}, u32[]{:S(2)}) copy-start(s32[4]{0:T(128)} %constant.62.clone) | copy-start | bytes 52
  103.8 35.9 %collective-permute-start.7 = (bf16[6144,128]{1,0:T(8,128)(2,1)}, bf16[6144,128]{1,0:T(8,128)(2,1)}, u32[]{:S(2)}, u32[]{:S(2)}) collective-permute-start(bf16[6144,128]{1,0:T(8,128)(2,1)} %get-tuple-element.66.refs_0_), channel_id=1, source_target_pairs={{24,8},{25,9},{16,0},{17,1},{18,2},{19,3},{26,10},{27,11},{12,28},... | collective-permute-start | bytes 4718600 | tf_op jit(solution)/shard_map/ppermute | solution.py:331
  108.8 38.8 %collective-permute-start.5 = (bf16[6144,128]{1,0:T(8,128)(2,1)}, bf16[6144,128]{1,0:T(8,128)(2,1)}, u32[]{:S(2)}, u32[]{:S(2)}) collective-permute-start(bf16[6144,128]{1,0:T(8,128)(2,1)} %get-tuple-element.63.refs_5_), channel_id=1, source_target_pairs={{2,0},{3,1},{4,6},{5,7},{10,8},{11,9},{12,14},{13,15},{18,16},{19,... | collective-permute-start | bytes 4718600 | tf_op jit(solution)/shard_map/ppermute | solution.py:331
  111.2 45.7 %collective-permute-start.6 = (bf16[6144,128]{1,0:T(8,128)(2,1)S(1)}, bf16[6144,128]{1,0:T(8,128)(2,1)}, u32[]{:S(2)}, u32[]{:S(2)}) collective-permute-start(bf16[6144,128]{1,0:T(8,128)(2,1)S(1)} %copy-done.2), channel_id=1, source_target_pairs={{2,4},{3,5},{4,2},{5,3},{10,12},{11,13},{12,10},{13,11},{18,20},{1... | collective-permute-start | bytes 4718600 | tf_op jit(solution)/shard_map/ppermute | solution.py:331
  128.3 46.5 %collective-permute-start.13 = (bf16[6144,128]{1,0:T(8,128)(2,1)}, bf16[6144,128]{1,0:T(8,128)(2,1)}, u32[]{:S(2)}, u32[]{:S(2)}) collective-permute-start(bf16[6144,128]{1,0:T(8,128)(2,1)} %get-tuple-element.77.refs_0_), channel_id=1, source_target_pairs={{16,24},{17,25},{0,8},{1,9},{26,18},{27,19},{10,2},{11,3},{4,12},{... | collective-permute-start | bytes 4718600 | tf_op jit(solution)/shard_map/ppermute | solution.py:331
  130.8 1.1 copy-start.3
  131.9 49.3 %collective-permute-start.12 = (bf16[6144,128]{1,0:T(8,128)(2,1)}, bf16[6144,128]{1,0:T(8,128)(2,1)S(1)}, u32[]{:S(2)}, u32[]{:S(2)}) collective-permute-start(bf16[6144,128]{1,0:T(8,128)(2,1)} %get-tuple-element.76.refs_3_), channel_id=1, source_target_pairs={{2,0},{3,1},{4,6},{5,7},{10,8},{11,9},{12,14},{13,15},{18,16},{19,... | collective-permute-start | bytes 4718600 | tf_op jit(solution)/shard_map/ppermute | solution.py:331
  143.1 58.0 %collective-permute-start.11 = (bf16[6144,128]{1,0:T(8,128)(2,1)}, bf16[6144,128]{1,0:T(8,128)(2,1)}, u32[]{:S(2)}, u32[]{:S(2)}) collective-permute-start(bf16[6144,128]{1,0:T(8,128)(2,1)} %get-tuple-element.75.refs_0_), channel_id=1, source_target_pairs={{8,0},{9,1},{2,10},{3,11},{28,20},{29,21},{22,30},{23,31}} | collective-permute-start | bytes 4718600 | tf_op jit(solution)/shard_map/ppermute | solution.py:331
  157.0 1.5 copy-start.14
  157.0 2.7 copy-start.13
  157.0 58.0 %collective-permute-start.10 = (bf16[6144,128]{1,0:T(8,128)(2,1)}, bf16[6144,128]{1,0:T(8,128)(2,1)S(1)}, u32[]{:S(2)}, u32[]{:S(2)}) collective-permute-start(bf16[6144,128]{1,0:T(8,128)(2,1)} %get-tuple-element.74.refs_3_), channel_id=1, source_target_pairs={{2,0},{3,1},{4,6},{5,7},{10,8},{11,9},{12,14},{13,15},{18,16},{19,... | collective-permute-start | bytes 4718600 | tf_op jit(solution)/shard_map/ppermute | solution.py:331
  181.3 1.2 copy-start.5
  182.4 16.9 %copy-start.6 = (bf16[6144,128]{1,0:T(8,128)(2,1)S(1)}, bf16[6144,128]{1,0:T(8,128)(2,1)}, u32[]{:S(2)}) copy-start(bf16[6144,128]{1,0:T(8,128)(2,1)} %get-tuple-element.94.refs_0_) | copy-start | bytes 4718596
  195.3 38.2 %collective-permute-start.18 = (bf16[3072,128]{1,0:T(8,128)(2,1)}, bf16[3072,128]{1,0:T(8,128)(2,1)}, u32[]{:S(2)}, u32[]{:S(2)}) collective-permute-start(bf16[3072,128]{1,0:T(8,128)(2,1)} %get-tuple-element.95.refs_0_), channel_id=1, source_target_pairs={{8,24},{9,25},{0,16},{1,17},{10,26},{11,27},{2,18},{3,19},{20,4},{... | collective-permute-start | bytes 2359304 | tf_op jit(solution)/shard_map/ppermute | solution.py:331
  196.6 38.4 %collective-permute-start.19 = (bf16[3072,128]{1,0:T(8,128)(2,1)}, bf16[3072,128]{1,0:T(8,128)(2,1)}, u32[]{:S(2)}, u32[]{:S(2)}) collective-permute-start(bf16[3072,128]{1,0:T(8,128)(2,1)} %get-tuple-element.96.refs_2_), channel_id=1, source_target_pairs={{8,0},{9,1},{24,16},{25,17},{10,2},{11,3},{26,18},{27,19},{20,28},... | collective-permute-start | bytes 2359304 | tf_op jit(solution)/shard_map/ppermute | solution.py:331
  199.3 38.6 %collective-permute-start.17 = (bf16[6144,128]{1,0:T(8,128)(2,1)S(1)}, bf16[6144,128]{1,0:T(8,128)(2,1)}, u32[]{:S(2)}, u32[]{:S(2)}) collective-permute-start(bf16[6144,128]{1,0:T(8,128)(2,1)S(1)} %copy-done.6), channel_id=1, source_target_pairs={{24,8},{25,9},{18,2},{19,3},{12,28},{13,29},{6,22},{7,23}} | collective-permute-start | bytes 4718600 | tf_op jit(solution)/shard_map/ppermute | solution.py:331
  204.1 59.3 %collective-permute-start.16 = (bf16[3072,128]{1,0:T(8,128)(2,1)}, bf16[3072,128]{1,0:T(8,128)(2,1)}, u32[]{:S(2)}, u32[]{:S(2)}) collective-permute-start(bf16[3072,128]{1,0:T(8,128)(2,1)} %get-tuple-element.93), channel_id=1, source_target_pairs={{0,1},{1,0},{2,3},{3,2},{4,5},{5,4},{6,7},{7,6},{8,9},{9,8},{10,11... | collective-permute-start | bytes 2359304 | tf_op jit(solution)/shard_map/ppermute | solution.py:331
  215.0 1.1 copy-start.4
  227.8 37.3 %collective-permute-start.14 = (bf16[3072,128]{1,0:T(8,128)(2,1)}, bf16[3072,128]{1,0:T(8,128)(2,1)S(1)}, u32[]{:S(2)}, u32[]{:S(2)}) collective-permute-start(bf16[3072,128]{1,0:T(8,128)(2,1)} %get-tuple-element.90.refs_0_), channel_id=1, source_target_pairs={{0,16},{1,17},{8,24},{9,25},{2,18},{3,19},{10,26},{11,27},{28,12},... | collective-permute-start | bytes 2359304 | tf_op jit(solution)/shard_map/ppermute | solution.py:331
  233.5 33.2 %collective-permute-start.15 = (bf16[3072,128]{1,0:T(8,128)(2,1)}, bf16[3072,128]{1,0:T(8,128)(2,1)S(1)}, u32[]{:S(2)}, u32[]{:S(2)}) collective-permute-start(bf16[3072,128]{1,0:T(8,128)(2,1)} %get-tuple-element.91.refs_2_), channel_id=1, source_target_pairs={{0,8},{1,9},{16,24},{17,25},{2,10},{3,11},{18,26},{19,27},{28,20},... | collective-permute-start | bytes 2359304 | tf_op jit(solution)/shard_map/ppermute | solution.py:331
  237.9 5.3 %copy-start.10 = (bf16[3072,128]{1,0:T(8,128)(2,1)S(1)}, bf16[3072,128]{1,0:T(8,128)(2,1)}, u32[]{:S(2)}) copy-start(bf16[3072,128]{1,0:T(8,128)(2,1)} %get-tuple-element.104.refs_0_) | copy-start | bytes 2359300
  241.0 34.3 %collective-permute-start.27 = (bf16[3072,128]{1,0:T(8,128)(2,1)}, bf16[3072,128]{1,0:T(8,128)(2,1)}, u32[]{:S(2)}, u32[]{:S(2)}) collective-permute-start(bf16[3072,128]{1,0:T(8,128)(2,1)} %get-tuple-element.107), channel_id=1, source_target_pairs={{0,1},{1,0},{2,3},{3,2},{4,5},{5,4},{6,7},{7,6},{8,9},{9,8},{10,11... | collective-permute-start | bytes 2359304 | tf_op jit(solution)/shard_map/ppermute | solution.py:331
  243.2 37.0 %collective-permute-start.24 = (bf16[3072,128]{1,0:T(8,128)(2,1)S(1)}, bf16[3072,128]{1,0:T(8,128)(2,1)S(1)}, u32[]{:S(2)}, u32[]{:S(2)}) collective-permute-start(bf16[3072,128]{1,0:T(8,128)(2,1)S(1)} %copy-done.10), channel_id=1, source_target_pairs={{24,16},{25,17},{26,18},{27,19},{4,12},{5,13},{6,14},{7,15}} | collective-permute-start | bytes 2359304 | tf_op jit(solution)/shard_map/ppermute | solution.py:331
  263.4 17.7 %collective-permute-start.25 = (bf16[3072,128]{1,0:T(8,128)(2,1)}, bf16[3072,128]{1,0:T(8,128)(2,1)}, u32[]{:S(2)}, u32[]{:S(2)}) collective-permute-start(bf16[3072,128]{1,0:T(8,128)(2,1)} %get-tuple-element.105), channel_id=1, source_target_pairs={{0,1},{1,0},{2,3},{3,2},{4,5},{5,4},{6,7},{7,6},{8,9},{9,8},{10,11... | collective-permute-start | bytes 2359304 | tf_op jit(solution)/shard_map/ppermute | solution.py:331
  265.1 1.6 copy-start.8
  265.1 22.2 %collective-permute-start.26 = (bf16[3072,128]{1,0:T(8,128)(2,1)}, bf16[3072,128]{1,0:T(8,128)(2,1)}, u32[]{:S(2)}, u32[]{:S(2)}) collective-permute-start(bf16[3072,128]{1,0:T(8,128)(2,1)} %get-tuple-element.105), channel_id=1, source_target_pairs={{0,17},{1,16},{2,19},{3,18},{28,13},{29,12},{30,15},{31,14}} | collective-permute-start | bytes 2359304 | tf_op jit(solution)/shard_map/ppermute | solution.py:331
  266.7 0.9 copy-start.9
  274.8 13.2 %collective-permute-start.23 = (bf16[3072,128]{1,0:T(8,128)(2,1)S(1)}, bf16[3072,128]{1,0:T(8,128)(2,1)S(1)}, u32[]{:S(2)}, u32[]{:S(2)}) collective-permute-start(bf16[3072,128]{1,0:T(8,128)(2,1)S(1)} %slice.12), channel_id=1, source_target_pairs={{0,1},{1,0},{2,3},{3,2},{4,5},{5,4},{6,7},{7,6},{8,9},{9,8},{10,11... | collective-permute-start | bytes 2359304 | tf_op jit(solution)/shard_map/ppermute | solution.py:331
  275.4 21.3 %collective-permute-start.20 = (bf16[3072,128]{1,0:T(8,128)(2,1)}, bf16[3072,128]{1,0:T(8,128)(2,1)}, u32[]{:S(2)}, u32[]{:S(2)}) collective-permute-start(bf16[3072,128]{1,0:T(8,128)(2,1)} %get-tuple-element.101.refs_0_), channel_id=1, source_target_pairs={{16,24},{17,25},{18,26},{19,27},{12,4},{13,5},{14,6},{15,7}} | collective-permute-start | bytes 2359304 | tf_op jit(solution)/shard_map/ppermute | solution.py:331
  280.2 7.1 %copy-start.11 = (bf16[3072,128]{1,0:T(8,128)(2,1)}, bf16[3072,128]{1,0:T(8,128)(2,1)S(1)}, u32[]{:S(2)}) copy-start(bf16[3072,128]{1,0:T(8,128)(2,1)S(1)} %collective-permute-done.24.refs_1_) | copy-start | bytes 2359300
  280.2 16.5 %collective-permute-start.21 = (bf16[3072,128]{1,0:T(8,128)(2,1)}, bf16[3072,128]{1,0:T(8,128)(2,1)S(1)}, u32[]{:S(2)}, u32[]{:S(2)}) collective-permute-start(bf16[3072,128]{1,0:T(8,128)(2,1)} %get-tuple-element.102), channel_id=1, source_target_pairs={{0,1},{1,0},{2,3},{3,2},{4,5},{5,4},{6,7},{7,6},{8,9},{9,8},{10,11... | collective-permute-start | bytes 2359304 | tf_op jit(solution)/shard_map/ppermute | solution.py:331
  281.0 21.4 %collective-permute-start.22 = (bf16[3072,128]{1,0:T(8,128)(2,1)}, bf16[3072,128]{1,0:T(8,128)(2,1)}, u32[]{:S(2)}, u32[]{:S(2)}) collective-permute-start(bf16[3072,128]{1,0:T(8,128)(2,1)} %get-tuple-element.102), channel_id=1, source_target_pairs={{8,25},{9,24},{10,27},{11,26},{20,5},{21,4},{22,7},{23,6}} | collective-permute-start | bytes 2359304 | tf_op jit(solution)/shard_map/ppermute | solution.py:331
  288.1 0.9 copy-start.7
  296.7 5.7 %copy-start.12 = (bf16[3072,128]{1,0:T(8,128)(2,1)}, bf16[3072,128]{1,0:T(8,128)(2,1)S(1)}, u32[]{:S(2)}) copy-start(bf16[3072,128]{1,0:T(8,128)(2,1)S(1)} %collective-permute-done.21.refs_2_) | copy-start | bytes 2359300
Sparse Core Ops, SparseCore 0:
  174.9 98.6 reduce-scatter.1

commit v3 on v2

--- a/solution.py
+++ b/solution.py
@@ -108,10 +108,12 @@
         return carry
 
     lax.fori_loop(0, (count + GROUP - 1) // GROUP, visit, 0)
-    result[...] = total[: result.shape[0], :].astype(result.dtype)
-    copies = []
+    copies, ready = [], set()
     for k, (start, size, top, height, target, tile) in enumerate(writes):
         there = pl.ds(pl.multiple_of(at_ref[tile], BLOCK) if tile else 0, height)
+        if (top, height) not in ready:
+            result[top : top + height, :] = total[top : top + height, :].astype(result.dtype)
+            ready.add((top, height))
         source = result.at[pl.ds(top, height), pl.ds(start, size)]
         copies.append(pltpu.make_async_copy(source, out_refs[target].at[there, :], out_sem.at[k]))
         copies[-1].start()

time: 316 us -> 315 us (level)
  starting transfers between devices: 65.6 us -> 69.5 us
    ppermute x28, starting transfers between devices: 65.6 us -> 69.5 us  [move(): return lax.ppermute(x, AXES, moves)]
    pallas_call x5, Pallas kernels: 64.4 us -> 60.9 us  [block_product(): pl.pallas_call(functools.partial(product_kernel, n_env, len(parts), len(o...]
  transfers between devices with their start and end apart: 29 -> 29, of which waited for: 14 -> 14; matrix products, arithmetic and copies ran while one was open for 4% -> 4% of each run, Pallas kernels for 34% -> 33%
where the time goes in v3:
time: 315 us; the launch traced here: 314 us
  Pallas kernels  108 us (34%)
  waiting for transfers between devices  101 us (32%)
  starting transfers between devices  69.5 us (22%)
  between operations  17.5 us (6%)
  local copies, waits for them, and re-layouts  12 us (4%)
  other arithmetic  5.6 us (2%)
    ppermute x28, waiting for transfers between devices, move(): return lax.ppermute(x, AXES, moves)  99.6 us
    ppermute x28, starting transfers between devices, move(): return lax.ppermute(x, AXES, moves)  69.5 us
    pallas_call x5, Pallas kernels, block_product(): pl.pallas_call(functools.partial(product_kernel, n_env, len(parts), len(o...  60.9 us
    pallas_call x1, Pallas kernels, block_pairs(): pl.pallas_call(functools.partial(pair_kernel, row_blocks, col_blocks), ou...  19.1 us
    pallas_call x6, Pallas kernels, add_pairs(): pl.pallas_call(functools.partial(add_kernel, count, parts), out_shape=[ja...  18.8 us
  transfers between devices with their start and end apart: 29, of which 14 were waited for; matrix products, arithmetic and copies ran while one was open for 4% of the time, Pallas kernels for 33%

profile of v3, /device:TPU:17, one launch (start us, length us, event | category | flops | bytes accessed | tf_op | source)
XLA Modules:
  0.0 313.6 jit_solution(9152847402993113889)
XLA Ops:
  6.5 0.7 collective-permute-start
  7.2 3.8 %fusion = (bf16[6144,128]{1,0:T(8,128)(2,1)}, bf16[6144,128]{1,0:T(8,128)(2,1)}) fusion(bf16[6144,256]{1,0:T(8,128)(2,1)} %refs_3_.1), kind=kLoop, calls=%fused_computation.9 | loop fusion | bytes 6291456 | tf_op jit(solution)/shard_map/slice | solution.py:341
  11.0 1.3 collective-permute-start.2
  12.3 1.9 collective-permute-start.3
  14.9 19.1 %block_pairs.1.refs_2_.pairs_ref = s32[617]{0:T(1024)} custom-call(s32[3]{0:T(128)} %pad_add_fusion.1.bases_ref, s32[96]{0:T(128)} %sectors_ref.1), custom_call_target="tpu_custom_call" | custom-call | flops 1 | bytes 1 | tf_op jit(solution)/shard_map/block_pairs/pallas_call | solution.py:37
  34.1 13.3 %collective-permute-done.2.refs_0_ = bf16[6144,128]{1,0:T(8,128)(2,1)S(1)} collective-permute-done((bf16[6144,128]{1,0:T(8,128)(2,1)}, bf16[6144,128]{1,0:T(8,128)(2,1)S(1)}, u32[]{:S(2)}, u32[]{:S(2)}) %collective-permute-start.2) | collective-permute-done | bytes 1572896 | tf_op jit(solution)/shard_map/ppermute | solution.py:333
  47.3 2.9 collective-permute-done.3.refs_1_
  50.2 2.2 collective-permute-start.4
  52.4 2.4 collective-permute-start.8
  54.9 26.2 %collective-permute-done.1.refs_0_ = bf16[6144,128]{1,0:T(8,128)(2,1)S(1)} collective-permute-done((bf16[6144,128]{1,0:T(8,128)(2,1)}, bf16[6144,128]{1,0:T(8,128)(2,1)S(1)}, u32[]{:S(2)}, u32[]{:S(2)}) %collective-permute-start.1) | collective-permute-done | bytes 1572896 | tf_op jit(solution)/shard_map/ppermute | solution.py:333
  81.0 6.1 %collective-permute-done.4.refs_1_ = bf16[6144,128]{1,0:T(8,128)(2,1)} collective-permute-done((bf16[6144,128]{1,0:T(8,128)(2,1)}, bf16[6144,128]{1,0:T(8,128)(2,1)}, u32[]{:S(2)}, u32[]{:S(2)}) %collective-permute-start.4) | collective-permute-done | bytes 1572896 | tf_op jit(solution)/shard_map/ppermute | solution.py:333
  87.2 2.6 collective-permute-start.9
  90.4 12.7 %block_product.5 = (bf16[24576,128]{1,0:T(8,128)(2,1)}, bf16[6144,128]{1,0:T(8,128)(2,1)}, f32[8,128]{1,0:T(8,128)}) custom-call(s32[617]{0:T(1024)} %block_pairs.1.refs_2_.pairs_ref, s32[2]{0:T(128)} %pad_add_fusion.2.at_ref, bf16[3072,6144]{1,0:T(8,128)(2,1)} %refs_0_.9, ...), custom_call_target="tpu_custom_call", output_to_operand_aliasing={{0}: (6, {})} | custom-call | flops 1 | bytes 1 | tf_op jit(solution)/shard_map/block_product/pallas_call | solution.py:127
  103.1 5.0 %collective-permute-start.7 = (bf16[6144,128]{1,0:T(8,128)(2,1)}, bf16[6144,128]{1,0:T(8,128)(2,1)}, u32[]{:S(2)}, u32[]{:S(2)}) collective-permute-start(bf16[6144,128]{1,0:T(8,128)(2,1)} %get-tuple-element.66.refs_0_), channel_id=1, source_target_pairs={{24,8},{25,9},{16,0},{17,1},{18,2},{19,3},{26,10},{27,11},{12,28},... | collective-permute-start | bytes 4718600 | tf_op jit(solution)/shard_map/ppermute | solution.py:333
  108.1 2.4 collective-permute-start.5
  110.5 1.9 collective-permute-start.6
  114.4 12.6 %block_product.6 = (bf16[24576,128]{1,0:T(8,128)(2,1)}, bf16[6144,128]{1,0:T(8,128)(2,1)}, f32[8,128]{1,0:T(8,128)}) custom-call(s32[617]{0:T(1024)} %block_pairs.1.refs_2_.pairs_ref, s32[2]{0:T(128)} %pad_add_fusion.3.at_ref, bf16[3072,6144]{1,0:T(8,128)(2,1)} %refs_0_.9, ...), custom_call_target="tpu_custom_call", output_to_operand_aliasing={{0}: (8, {})} | custom-call | flops 1 | bytes 1 | tf_op jit(solution)/shard_map/block_product/pallas_call | solution.py:127
  126.9 3.6 %collective-permute-start.13 = (bf16[6144,128]{1,0:T(8,128)(2,1)}, bf16[6144,128]{1,0:T(8,128)(2,1)}, u32[]{:S(2)}, u32[]{:S(2)}) collective-permute-start(bf16[6144,128]{1,0:T(8,128)(2,1)} %get-tuple-element.77.refs_0_), channel_id=1, source_target_pairs={{16,24},{17,25},{0,8},{1,9},{26,18},{27,19},{10,2},{11,3},{4,12},{... | collective-permute-start | bytes 4718600 | tf_op jit(solution)/shard_map/ppermute | solution.py:333
  130.5 1.1 copy-done.3
  131.7 1.4 collective-permute-start.12
  133.0 5.9 %collective-permute-done.7.refs_1_ = bf16[6144,128]{1,0:T(8,128)(2,1)} collective-permute-done((bf16[6144,128]{1,0:T(8,128)(2,1)}, bf16[6144,128]{1,0:T(8,128)(2,1)}, u32[]{:S(2)}, u32[]{:S(2)}) %collective-permute-start.7) | collective-permute-done | bytes 1572896 | tf_op jit(solution)/shard_map/ppermute | solution.py:333
  139.0 3.4 %add_pairs.6 = (bf16[6144,128]{1,0:T(8,128)(2,1)}, f32[8,128]{1,0:T(8,128)}) custom-call(bf16[6144,128]{1,0:T(8,128)(2,1)} %get-tuple-element.66.refs_0_, bf16[6144,128]{1,0:T(8,128)(2,1)} %collective-permute-done.7.refs_1_, f32[8,128]{1,0:T(8,128)} %get-tuple-element.72.refs_2_), custom_call_target="tpu_custom_call" | custom-call | flops 1 | bytes 1 | tf_op jit(solution)/shard_map/add_pairs/pallas_call | solution.py:191
  142.4 1.8 collective-permute-start.11
  144.3 3.3 %collective-permute-done.5.refs_0_ = bf16[6144,128]{1,0:T(8,128)(2,1)} collective-permute-done((bf16[6144,128]{1,0:T(8,128)(2,1)}, bf16[6144,128]{1,0:T(8,128)(2,1)}, u32[]{:S(2)}, u32[]{:S(2)}) %collective-permute-start.5) | collective-permute-done | bytes 1572896 | tf_op jit(solution)/shard_map/ppermute | solution.py:333
  147.5 9.4 %collective-permute-done.6.refs_1_ = bf16[6144,128]{1,0:T(8,128)(2,1)} collective-permute-done((bf16[6144,128]{1,0:T(8,128)(2,1)S(1)}, bf16[6144,128]{1,0:T(8,128)(2,1)}, u32[]{:S(2)}, u32[]{:S(2)}) %collective-permute-start.6) | collective-permute-done | bytes 1572896 | tf_op jit(solution)/shard_map/ppermute | solution.py:333
  157.0 1.5 collective-permute-start.10
  160.9 0.7 pad_add_fusion.4.at_ref
  161.6 12.5 %block_product.7 = (bf16[24576,128]{1,0:T(8,128)(2,1)}, f32[8,128]{1,0:T(8,128)}) custom-call(s32[617]{0:T(1024)} %block_pairs.1.refs_2_.pairs_ref, s32[3]{0:T(128)} %pad_add_fusion.4.at_ref, bf16[3072,6144]{1,0:T(8,128)(2,1)} %refs_0_.9, bf16[3072,6144]{1,0:T(8,128)(2,1)} %collective-permute-done.refs_1_, ...), custom_call_target="tpu_custom_call", output_to_operand_aliasing={{0}: (8, {})} | custom-call | flops 1 | bytes 1 | tf_op jit(solution)/shard_map/block_product/pallas_call | solution.py:127
  174.1 3.4 %add_pairs.7 = (bf16[6144,128]{1,0:T(8,128)(2,1)}, f32[8,128]{1,0:T(8,128)}) custom-call(bf16[6144,128]{1,0:T(8,128)(2,1)} %get-tuple-element.77.refs_0_, bf16[6144,128]{1,0:T(8,128)(2,1)} %collective-permute-done.13.refs_1_, f32[8,128]{1,0:T(8,128)} %get-tuple-element.82.refs_2_), custom_call_target="tpu_custom_call" | custom-call | flops 1 | bytes 1 | tf_op jit(solution)/shard_map/add_pairs/pallas_call | solution.py:191
  177.5 3.7 %collective-permute-done.12.refs_0_ = bf16[6144,128]{1,0:T(8,128)(2,1)S(1)} collective-permute-done((bf16[6144,128]{1,0:T(8,128)(2,1)}, bf16[6144,128]{1,0:T(8,128)(2,1)S(1)}, u32[]{:S(2)}, u32[]{:S(2)}) %collective-permute-start.12) | collective-permute-done | bytes 1572896 | tf_op jit(solution)/shard_map/ppermute | solution.py:333
  181.3 1.1 copy-done.5
  182.4 12.2 %block_product.8 = (bf16[3072,128]{1,0:T(8,128)(2,1)}, bf16[3072,128]{1,0:T(8,128)(2,1)}, f32[8,128]{1,0:T(8,128)}) custom-call(s32[617]{0:T(1024)} %block_pairs.1.refs_2_.pairs_ref, s32[1]{0:T(128)} %bitcast.6.at_ref, bf16[3072,6144]{1,0:T(8,128)(2,1)} %refs_0_.9, bf16[3072,6144]{1,0:T(8,128)(2,1)} %collective-permute-done.refs_1_, ...), custom_call_target="tpu_custom_call" | custom-call | flops 1 | bytes 1 | tf_op jit(solution)/shard_map/block_product/pallas_call | solution.py:127
  194.6 1.3 collective-permute-start.18
  195.9 4.0 %collective-permute-start.19 = (bf16[3072,128]{1,0:T(8,128)(2,1)}, bf16[3072,128]{1,0:T(8,128)(2,1)}, u32[]{:S(2)}, u32[]{:S(2)}) collective-permute-start(bf16[3072,128]{1,0:T(8,128)(2,1)} %get-tuple-element.96.refs_2_), channel_id=1, source_target_pairs={{8,0},{9,1},{24,16},{25,17},{10,2},{11,3},{26,18},{27,19},{20,28},... | collective-permute-start | bytes 2359304 | tf_op jit(solution)/shard_map/ppermute | solution.py:333
  199.9 1.8 collective-permute-start.17
  201.7 3.0 add_pairs.8
  204.7 1.2 collective-permute-start.16
  205.9 9.1 %collective-permute-done.10.refs_0_ = bf16[6144,128]{1,0:T(8,128)(2,1)S(1)} collective-permute-done((bf16[6144,128]{1,0:T(8,128)(2,1)}, bf16[6144,128]{1,0:T(8,128)(2,1)S(1)}, u32[]{:S(2)}, u32[]{:S(2)}) %collective-permute-start.10) | collective-permute-done | bytes 1572896 | tf_op jit(solution)/shard_map/ppermute | solution.py:333
  215.0 1.1 copy-done.4
  216.1 11.0 %block_product.9 = (bf16[3072,128]{1,0:T(8,128)(2,1)}, bf16[3072,128]{1,0:T(8,128)(2,1)}, f32[8,128]{1,0:T(8,128)}) custom-call(s32[617]{0:T(1024)} %block_pairs.1.refs_2_.pairs_ref, s32[1]{0:T(128)} %bitcast.6.at_ref, bf16[3072,6144]{1,0:T(8,128)(2,1)} %refs_0_.9, bf16[3072,6144]{1,0:T(8,128)(2,1)} %collective-permute-done.refs_1_, ...), custom_call_target="tpu_custom_call" | custom-call | flops 1 | bytes 1 | tf_op jit(solution)/shard_map/block_product/pallas_call | solution.py:127
  227.1 1.3 collective-permute-start.14
  228.4 4.4 %collective-permute-done.18.refs_1_ = bf16[3072,128]{1,0:T(8,128)(2,1)} collective-permute-done((bf16[3072,128]{1,0:T(8,128)(2,1)}, bf16[3072,128]{1,0:T(8,128)(2,1)}, u32[]{:S(2)}, u32[]{:S(2)}) %collective-permute-start.18) | collective-permute-done | bytes 786464 | tf_op jit(solution)/shard_map/ppermute | solution.py:333
  232.8 1.5 collective-permute-start.15
  234.3 3.0 add_pairs.9
  237.3 3.0 add_pairs.10
  240.3 2.0 collective-permute-start.27
  242.3 21.7 %collective-permute-start.24 = (bf16[3072,128]{1,0:T(8,128)(2,1)S(1)}, bf16[3072,128]{1,0:T(8,128)(2,1)S(1)}, u32[]{:S(2)}, u32[]{:S(2)}) collective-permute-start(bf16[3072,128]{1,0:T(8,128)(2,1)S(1)} %copy-done.10), channel_id=1, source_target_pairs={{24,16},{25,17},{26,18},{27,19},{4,12},{5,13},{6,14},{7,15}} | collective-permute-start | bytes 2359304 | tf_op jit(solution)/shard_map/ppermute | solution.py:333
  265.1 0.7 place_set.3
  265.8 1.5 collective-permute-start.26
  267.4 0.9 copy-done.9
  268.3 3.0 add_pairs.11
  271.3 1.7 reduce-scatter.2.cloned.1.call-done.own_ref
  272.9 1.2 slice.12
  274.7 1.3 collective-permute-start.20
  276.0 4.9 %collective-permute-done.24.refs_1_ = bf16[3072,128]{1,0:T(8,128)(2,1)S(1)} collective-permute-done((bf16[3072,128]{1,0:T(8,128)(2,1)S(1)}, bf16[3072,128]{1,0:T(8,128)(2,1)S(1)}, u32[]{:S(2)}, u32[]{:S(2)}) %collective-permute-start.24) | collective-permute-done | bytes 786464 | tf_op jit(solution)/shard_map/ppermute | solution.py:333
  280.9 0.8 collective-permute-start.21
  281.7 1.3 collective-permute-start.22
  287.3 0.7 place_set.4
  288.0 0.7 place.2
  288.8 0.9 copy-done.7
  289.7 3.0 place_set.5
  292.7 3.3 %collective-permute-done.20.refs_1_ = bf16[3072,128]{1,0:T(8,128)(2,1)} collective-permute-done((bf16[3072,128]{1,0:T(8,128)(2,1)}, bf16[3072,128]{1,0:T(8,128)(2,1)}, u32[]{:S(2)}, u32[]{:S(2)}) %collective-permute-start.20) | collective-permute-done | bytes 786464 | tf_op jit(solution)/shard_map/ppermute | solution.py:333
  296.0 7.1 %collective-permute-done.22.refs_3_ = bf16[3072,128]{1,0:T(8,128)(2,1)} collective-permute-done((bf16[3072,128]{1,0:T(8,128)(2,1)}, bf16[3072,128]{1,0:T(8,128)(2,1)}, u32[]{:S(2)}, u32[]{:S(2)}) %collective-permute-start.22) | collective-permute-done | bytes 786464 | tf_op jit(solution)/shard_map/ppermute | solution.py:333
  303.1 3.6 %place.3 = (bf16[3072,512]{1,0:T(8,128)(2,1)}, f32[8,128]{1,0:T(8,128)}) custom-call(s32[2]{0:T(128)} %pad_add_fusion.flags_ref, bf16[3072,128]{1,0:T(8,128)(2,1)} %get-tuple-element.101.refs_0_, bf16[3072,128]{1,0:T(8,128)(2,1)} %collective-permute-done.20.refs_1_, bf16[3072,128]{1,0:T(8,128)(2,1)} %copy-done.12, ...), custom_call_target="tpu_custom_call", output_to_operand_aliasing={{0}: (5, {})} | custom-call | flops 1 | bytes 1 | tf_op jit(solution)/shard_map/place/pallas_call | solution.py:234
  (66 shorter events, 7.9 us)
Async XLA Ops:
  6.5 266.4 %reduce-scatter.2.cloned.1.call-start = ((), (), s32[]{:S(2)}) async-start(), calls=%async_computation.1 | async-start | bytes 7864320 | tf_op jit(solution)/shard_map/reduce_scatter | solution.py:416
  6.5 83.9 %collective-permute-start = (bf16[3072,6144]{1,0:T(8,128)(2,1)}, bf16[3072,6144]{1,0:T(8,128)(2,1)}, u32[]{:S(2)}, u32[]{:S(2)}) collective-permute-start(bf16[3072,6144]{1,0:T(8,128)(2,1)} %refs_0_.9), channel_id=1, source_target_pairs={{0,1},{1,0},{2,3},{3,2},{4,5},{5,4},{6,7},{7,6},{8,9},{9,8},{10,11... | collective-permute-start | bytes 113246216 | tf_op jit(solution)/shard_map/ppermute | solution.py:333
  11.0 36.3 %collective-permute-start.2 = (bf16[6144,128]{1,0:T(8,128)(2,1)}, bf16[6144,128]{1,0:T(8,128)(2,1)S(1)}, u32[]{:S(2)}, u32[]{:S(2)}) collective-permute-start(bf16[6144,128]{1,0:T(8,128)(2,1)} %get-tuple-element.117), channel_id=1, source_target_pairs={{0,2},{1,3},{2,0},{3,1},{4,6},{5,7},{6,4},{7,5},{8,10},{9,11},{10,... | collective-permute-start | bytes 4718600 | tf_op jit(solution)/shard_map/ppermute | solution.py:333
  12.3 37.9 %collective-permute-start.3 = (bf16[6144,128]{1,0:T(8,128)(2,1)}, bf16[6144,128]{1,0:T(8,128)(2,1)}, u32[]{:S(2)}, u32[]{:S(2)}) collective-permute-start(bf16[6144,128]{1,0:T(8,128)(2,1)} %get-tuple-element.117), channel_id=1, source_target_pairs={{2,4},{3,5},{4,2},{5,3},{10,12},{11,13},{12,10},{13,11},{18,20},{1... | collective-permute-start | bytes 4718600 | tf_op jit(solution)/shard_map/ppermute | solution.py:333
  14.2 66.8 %collective-permute-start.1 = (bf16[6144,128]{1,0:T(8,128)(2,1)}, bf16[6144,128]{1,0:T(8,128)(2,1)S(1)}, u32[]{:S(2)}, u32[]{:S(2)}) collective-permute-start(bf16[6144,128]{1,0:T(8,128)(2,1)} %get-tuple-element.118.refs_2_), channel_id=1, source_target_pairs={{0,2},{1,3},{2,0},{3,1},{4,6},{5,7},{6,4},{7,5},{8,10},{9,11},{10,... | collective-permute-start | bytes 4718600 | tf_op jit(solution)/shard_map/ppermute | solution.py:333
  47.3 2.9 copy-start
  50.2 37.0 %collective-permute-start.4 = (bf16[6144,128]{1,0:T(8,128)(2,1)}, bf16[6144,128]{1,0:T(8,128)(2,1)}, u32[]{:S(2)}, u32[]{:S(2)}) collective-permute-start(bf16[6144,128]{1,0:T(8,128)(2,1)} %get-tuple-element.61.refs_2_.refs_3_), channel_id=1, source_target_pairs={{2,4},{3,5},{4,2},{5,3},{10,12},{11,13},{12,10},{13,11},{18,20},{1... | collective-permute-start | bytes 4718600 | tf_op jit(solution)/shard_map/ppermute | solution.py:333
  52.4 74.5 %collective-permute-start.8 = (bf16[6144,128]{1,0:T(8,128)(2,1)}, bf16[6144,128]{1,0:T(8,128)(2,1)}, u32[]{:S(2)}, u32[]{:S(2)}) collective-permute-start(bf16[6144,128]{1,0:T(8,128)(2,1)} %get-tuple-element.67.refs_3_), channel_id=1, source_target_pairs={{2,0},{3,1},{4,6},{5,7},{10,8},{11,9},{12,14},{13,15},{18,16},{19,... | collective-permute-start | bytes 4718600 | tf_op jit(solution)/shard_map/ppermute | solution.py:333
  81.0 6.1 %copy-start.1 = (bf16[6144,128]{1,0:T(8,128)(2,1)}, bf16[6144,128]{1,0:T(8,128)(2,1)S(1)}, u32[]{:S(2)}) copy-start(bf16[6144,128]{1,0:T(8,128)(2,1)S(1)} %collective-permute-done.1.refs_0_) | copy-start | bytes 4718596
  87.2 43.3 %collective-permute-start.9 = (bf16[6144,128]{1,0:T(8,128)(2,1)}, bf16[6144,128]{1,0:T(8,128)(2,1)S(1)}, u32[]{:S(2)}, u32[]{:S(2)}) collective-permute-start(bf16[6144,128]{1,0:T(8,128)(2,1)} %get-tuple-element.68), channel_id=1, source_target_pairs={{2,4},{3,5},{4,2},{5,3},{10,12},{11,13},{12,10},{13,11},{18,20},{1... | collective-permute-start | bytes 4718600 | tf_op jit(solution)/shard_map/ppermute | solution.py:333
  90.4 20.1 %copy-start.2 = (bf16[6144,128]{1,0:T(8,128)(2,1)S(1)}, bf16[6144,128]{1,0:T(8,128)(2,1)}, u32[]{:S(2)}) copy-start(bf16[6144,128]{1,0:T(8,128)(2,1)} %get-tuple-element.64.refs_4_.refs_5_) | copy-start | bytes 4718596
  90.4 22.0 %copy-start.15 = (s32[4]{0:T(128)S(1)}, s32[4]{0:T(128)}, u32[]{:S(2)}) copy-start(s32[4]{0:T(128)} %constant.62.clone) | copy-start | bytes 52
  103.1 35.9 %collective-permute-start.7 = (bf16[6144,128]{1,0:T(8,128)(2,1)}, bf16[6144,128]{1,0:T(8,128)(2,1)}, u32[]{:S(2)}, u32[]{:S(2)}) collective-permute-start(bf16[6144,128]{1,0:T(8,128)(2,1)} %get-tuple-element.66.refs_0_), channel_id=1, source_target_pairs={{24,8},{25,9},{16,0},{17,1},{18,2},{19,3},{26,10},{27,11},{12,28},... | collective-permute-start | bytes 4718600 | tf_op jit(solution)/shard_map/ppermute | solution.py:333
  108.1 39.4 %collective-permute-start.5 = (bf16[6144,128]{1,0:T(8,128)(2,1)}, bf16[6144,128]{1,0:T(8,128)(2,1)}, u32[]{:S(2)}, u32[]{:S(2)}) collective-permute-start(bf16[6144,128]{1,0:T(8,128)(2,1)} %get-tuple-element.63.refs_5_), channel_id=1, source_target_pairs={{2,0},{3,1},{4,6},{5,7},{10,8},{11,9},{12,14},{13,15},{18,16},{19,... | collective-permute-start | bytes 4718600 | tf_op jit(solution)/shard_map/ppermute | solution.py:333
  110.5 46.4 %collective-permute-start.6 = (bf16[6144,128]{1,0:T(8,128)(2,1)S(1)}, bf16[6144,128]{1,0:T(8,128)(2,1)}, u32[]{:S(2)}, u32[]{:S(2)}) collective-permute-start(bf16[6144,128]{1,0:T(8,128)(2,1)S(1)} %copy-done.2), channel_id=1, source_target_pairs={{2,4},{3,5},{4,2},{5,3},{10,12},{11,13},{12,10},{13,11},{18,20},{1... | collective-permute-start | bytes 4718600 | tf_op jit(solution)/shard_map/ppermute | solution.py:333
  126.9 47.2 %collective-permute-start.13 = (bf16[6144,128]{1,0:T(8,128)(2,1)}, bf16[6144,128]{1,0:T(8,128)(2,1)}, u32[]{:S(2)}, u32[]{:S(2)}) collective-permute-start(bf16[6144,128]{1,0:T(8,128)(2,1)} %get-tuple-element.77.refs_0_), channel_id=1, source_target_pairs={{16,24},{17,25},{0,8},{1,9},{26,18},{27,19},{10,2},{11,3},{4,12},{... | collective-permute-start | bytes 4718600 | tf_op jit(solution)/shard_map/ppermute | solution.py:333
  130.5 1.1 copy-start.3
  131.7 49.6 %collective-permute-start.12 = (bf16[6144,128]{1,0:T(8,128)(2,1)}, bf16[6144,128]{1,0:T(8,128)(2,1)S(1)}, u32[]{:S(2)}, u32[]{:S(2)}) collective-permute-start(bf16[6144,128]{1,0:T(8,128)(2,1)} %get-tuple-element.76.refs_3_), channel_id=1, source_target_pairs={{2,0},{3,1},{4,6},{5,7},{10,8},{11,9},{12,14},{13,15},{18,16},{19,... | collective-permute-start | bytes 4718600 | tf_op jit(solution)/shard_map/ppermute | solution.py:333
  142.4 59.3 %collective-permute-start.11 = (bf16[6144,128]{1,0:T(8,128)(2,1)}, bf16[6144,128]{1,0:T(8,128)(2,1)}, u32[]{:S(2)}, u32[]{:S(2)}) collective-permute-start(bf16[6144,128]{1,0:T(8,128)(2,1)} %get-tuple-element.75.refs_0_), channel_id=1, source_target_pairs={{8,0},{9,1},{2,10},{3,11},{28,20},{29,21},{22,30},{23,31}} | collective-permute-start | bytes 4718600 | tf_op jit(solution)/shard_map/ppermute | solution.py:333
  157.0 1.5 copy-start.14
  157.0 2.7 copy-start.13
  157.0 58.0 %collective-permute-start.10 = (bf16[6144,128]{1,0:T(8,128)(2,1)}, bf16[6144,128]{1,0:T(8,128)(2,1)S(1)}, u32[]{:S(2)}, u32[]{:S(2)}) collective-permute-start(bf16[6144,128]{1,0:T(8,128)(2,1)} %get-tuple-element.74.refs_3_), channel_id=1, source_target_pairs={{2,0},{3,1},{4,6},{5,7},{10,8},{11,9},{12,14},{13,15},{18,16},{19,... | collective-permute-start | bytes 4718600 | tf_op jit(solution)/shard_map/ppermute | solution.py:333
  181.3 1.2 copy-start.5
  182.4 17.5 %copy-start.6 = (bf16[6144,128]{1,0:T(8,128)(2,1)S(1)}, bf16[6144,128]{1,0:T(8,128)(2,1)}, u32[]{:S(2)}) copy-start(bf16[6144,128]{1,0:T(8,128)(2,1)} %get-tuple-element.94.refs_0_) | copy-start | bytes 4718596
  194.6 38.2 %collective-permute-start.18 = (bf16[3072,128]{1,0:T(8,128)(2,1)}, bf16[3072,128]{1,0:T(8,128)(2,1)}, u32[]{:S(2)}, u32[]{:S(2)}) collective-permute-start(bf16[3072,128]{1,0:T(8,128)(2,1)} %get-tuple-element.95.refs_0_), channel_id=1, source_target_pairs={{8,24},{9,25},{0,16},{1,17},{10,26},{11,27},{2,18},{3,19},{20,4},{... | collective-permute-start | bytes 2359304 | tf_op jit(solution)/shard_map/ppermute | solution.py:333
  195.9 38.4 %collective-permute-start.19 = (bf16[3072,128]{1,0:T(8,128)(2,1)}, bf16[3072,128]{1,0:T(8,128)(2,1)}, u32[]{:S(2)}, u32[]{:S(2)}) collective-permute-start(bf16[3072,128]{1,0:T(8,128)(2,1)} %get-tuple-element.96.refs_2_), channel_id=1, source_target_pairs={{8,0},{9,1},{24,16},{25,17},{10,2},{11,3},{26,18},{27,19},{20,28},... | collective-permute-start | bytes 2359304 | tf_op jit(solution)/shard_map/ppermute | solution.py:333
  199.9 37.3 %collective-permute-start.17 = (bf16[6144,128]{1,0:T(8,128)(2,1)S(1)}, bf16[6144,128]{1,0:T(8,128)(2,1)}, u32[]{:S(2)}, u32[]{:S(2)}) collective-permute-start(bf16[6144,128]{1,0:T(8,128)(2,1)S(1)} %copy-done.6), channel_id=1, source_target_pairs={{24,8},{25,9},{18,2},{19,3},{12,28},{13,29},{6,22},{7,23}} | collective-permute-start | bytes 4718600 | tf_op jit(solution)/shard_map/ppermute | solution.py:333
  204.7 59.3 %collective-permute-start.16 = (bf16[3072,128]{1,0:T(8,128)(2,1)}, bf16[3072,128]{1,0:T(8,128)(2,1)}, u32[]{:S(2)}, u32[]{:S(2)}) collective-permute-start(bf16[3072,128]{1,0:T(8,128)(2,1)} %get-tuple-element.93), channel_id=1, source_target_pairs={{0,1},{1,0},{2,3},{3,2},{4,5},{5,4},{6,7},{7,6},{8,9},{9,8},{10,11... | collective-permute-start | bytes 2359304 | tf_op jit(solution)/shard_map/ppermute | solution.py:333
  215.0 1.1 copy-start.4
  227.1 38.7 %collective-permute-start.14 = (bf16[3072,128]{1,0:T(8,128)(2,1)}, bf16[3072,128]{1,0:T(8,128)(2,1)S(1)}, u32[]{:S(2)}, u32[]{:S(2)}) collective-permute-start(bf16[3072,128]{1,0:T(8,128)(2,1)} %get-tuple-element.90.refs_0_), channel_id=1, source_target_pairs={{0,16},{1,17},{8,24},{9,25},{2,18},{3,19},{10,26},{11,27},{28,12},... | collective-permute-start | bytes 2359304 | tf_op jit(solution)/shard_map/ppermute | solution.py:333
  232.8 34.6 %collective-permute-start.15 = (bf16[3072,128]{1,0:T(8,128)(2,1)}, bf16[3072,128]{1,0:T(8,128)(2,1)S(1)}, u32[]{:S(2)}, u32[]{:S(2)}) collective-permute-start(bf16[3072,128]{1,0:T(8,128)(2,1)} %get-tuple-element.91.refs_2_), channel_id=1, source_target_pairs={{0,8},{1,9},{16,24},{17,25},{2,10},{3,11},{18,26},{19,27},{28,20},... | collective-permute-start | bytes 2359304 | tf_op jit(solution)/shard_map/ppermute | solution.py:333
  237.2 5.1 %copy-start.10 = (bf16[3072,128]{1,0:T(8,128)(2,1)S(1)}, bf16[3072,128]{1,0:T(8,128)(2,1)}, u32[]{:S(2)}) copy-start(bf16[3072,128]{1,0:T(8,128)(2,1)} %get-tuple-element.104.refs_0_) | copy-start | bytes 2359300
  240.3 34.4 %collective-permute-start.27 = (bf16[3072,128]{1,0:T(8,128)(2,1)}, bf16[3072,128]{1,0:T(8,128)(2,1)}, u32[]{:S(2)}, u32[]{:S(2)}) collective-permute-start(bf16[3072,128]{1,0:T(8,128)(2,1)} %get-tuple-element.107), channel_id=1, source_target_pairs={{0,1},{1,0},{2,3},{3,2},{4,5},{5,4},{6,7},{7,6},{8,9},{9,8},{10,11... | collective-permute-start | bytes 2359304 | tf_op jit(solution)/shard_map/ppermute | solution.py:333
  242.3 38.6 %collective-permute-start.24 = (bf16[3072,128]{1,0:T(8,128)(2,1)S(1)}, bf16[3072,128]{1,0:T(8,128)(2,1)S(1)}, u32[]{:S(2)}, u32[]{:S(2)}) collective-permute-start(bf16[3072,128]{1,0:T(8,128)(2,1)S(1)} %copy-done.10), channel_id=1, source_target_pairs={{24,16},{25,17},{26,18},{27,19},{4,12},{5,13},{6,14},{7,15}} | collective-permute-start | bytes 2359304 | tf_op jit(solution)/shard_map/ppermute | solution.py:333
  264.0 17.7 %collective-permute-start.25 = (bf16[3072,128]{1,0:T(8,128)(2,1)}, bf16[3072,128]{1,0:T(8,128)(2,1)}, u32[]{:S(2)}, u32[]{:S(2)}) collective-permute-start(bf16[3072,128]{1,0:T(8,128)(2,1)} %get-tuple-element.105), channel_id=1, source_target_pairs={{0,1},{1,0},{2,3},{3,2},{4,5},{5,4},{6,7},{7,6},{8,9},{9,8},{10,11... | collective-permute-start | bytes 2359304 | tf_op jit(solution)/shard_map/ppermute | solution.py:333
  265.8 1.6 copy-start.8
  265.8 22.2 %collective-permute-start.26 = (bf16[3072,128]{1,0:T(8,128)(2,1)}, bf16[3072,128]{1,0:T(8,128)(2,1)}, u32[]{:S(2)}, u32[]{:S(2)}) collective-permute-start(bf16[3072,128]{1,0:T(8,128)(2,1)} %get-tuple-element.105), channel_id=1, source_target_pairs={{0,17},{1,16},{2,19},{3,18},{28,13},{29,12},{30,15},{31,14}} | collective-permute-start | bytes 2359304 | tf_op jit(solution)/shard_map/ppermute | solution.py:333
  267.4 0.9 copy-start.9
  274.1 14.6 %collective-permute-start.23 = (bf16[3072,128]{1,0:T(8,128)(2,1)S(1)}, bf16[3072,128]{1,0:T(8,128)(2,1)S(1)}, u32[]{:S(2)}, u32[]{:S(2)}) collective-permute-start(bf16[3072,128]{1,0:T(8,128)(2,1)S(1)} %slice.12), channel_id=1, source_target_pairs={{0,1},{1,0},{2,3},{3,2},{4,5},{5,4},{6,7},{7,6},{8,9},{9,8},{10,11... | collective-permute-start | bytes 2359304 | tf_op jit(solution)/shard_map/ppermute | solution.py:333
  274.7 21.3 %collective-permute-start.20 = (bf16[3072,128]{1,0:T(8,128)(2,1)}, bf16[3072,128]{1,0:T(8,128)(2,1)}, u32[]{:S(2)}, u32[]{:S(2)}) collective-permute-start(bf16[3072,128]{1,0:T(8,128)(2,1)} %get-tuple-element.101.refs_0_), channel_id=1, source_target_pairs={{16,24},{17,25},{18,26},{19,27},{12,4},{13,5},{14,6},{15,7}} | collective-permute-start | bytes 2359304 | tf_op jit(solution)/shard_map/ppermute | solution.py:333
  280.9 7.1 %copy-start.11 = (bf16[3072,128]{1,0:T(8,128)(2,1)}, bf16[3072,128]{1,0:T(8,128)(2,1)S(1)}, u32[]{:S(2)}) copy-start(bf16[3072,128]{1,0:T(8,128)(2,1)S(1)} %collective-permute-done.24.refs_1_) | copy-start | bytes 2359300
  280.9 15.1 %collective-permute-start.21 = (bf16[3072,128]{1,0:T(8,128)(2,1)}, bf16[3072,128]{1,0:T(8,128)(2,1)S(1)}, u32[]{:S(2)}, u32[]{:S(2)}) collective-permute-start(bf16[3072,128]{1,0:T(8,128)(2,1)} %get-tuple-element.102), channel_id=1, source_target_pairs={{0,1},{1,0},{2,3},{3,2},{4,5},{5,4},{6,7},{7,6},{8,9},{9,8},{10,11... | collective-permute-start | bytes 2359304 | tf_op jit(solution)/shard_map/ppermute | solution.py:333
  281.7 21.4 %collective-permute-start.22 = (bf16[3072,128]{1,0:T(8,128)(2,1)}, bf16[3072,128]{1,0:T(8,128)(2,1)}, u32[]{:S(2)}, u32[]{:S(2)}) collective-permute-start(bf16[3072,128]{1,0:T(8,128)(2,1)} %get-tuple-element.102), channel_id=1, source_target_pairs={{8,25},{9,24},{10,27},{11,26},{20,5},{21,4},{22,7},{23,6}} | collective-permute-start | bytes 2359304 | tf_op jit(solution)/shard_map/ppermute | solution.py:333
  288.8 0.9 copy-start.7
  296.0 7.1 %copy-start.12 = (bf16[3072,128]{1,0:T(8,128)(2,1)}, bf16[3072,128]{1,0:T(8,128)(2,1)S(1)}, u32[]{:S(2)}) copy-start(bf16[3072,128]{1,0:T(8,128)(2,1)S(1)} %collective-permute-done.21.refs_2_) | copy-start | bytes 2359300
Sparse Core Ops, SparseCore 0:
  174.2 98.6 reduce-scatter.1
